TPU v7x, 256 devices: a whole 4x4x8 slice. The times are simulated.
256 devices in a mesh: dp: 32 (over z, x_hi, core), tensor: 8 (over y, x_lo).
Axes of the slice: x: 4 (x_hi: 2, x_lo: 2; x = x_hi * 2 + x_lo), y: 4, z: 8, core: 2. Of those that a mesh axis runs over, the one named last changes fastest.
Arguments:
- queries: bfloat16 [32768, 4096], P(('dp', 'tensor')), parts along dimension 0, may hold values from -120 to 120
- keys: bfloat16 [32768, 4096], P(('dp', 'tensor')), parts along dimension 0, may hold values from -8 to 8
- values: bfloat16 [32768, 4096], P(('dp', 'tensor')), parts along dimension 0, may hold values from -30 to 30
- segment_ids: int32 [32768], P('dp'), parts along dimension 0, may hold values from 0 to 3, never falling along the last dimension, each value on 1 to 512 neighbouring positions
- residual: bfloat16 [32768, 4096], P(('dp', 'tensor')), parts along dimension 0, may hold values from -6 to 6
- sub_gain: float32 [4096], P('tensor'), may hold values from 0.25 to 1.75
- sub_bias: float32 [4096], P('tensor'), may hold values from -3 to 3
- out_weight: bfloat16 [4096, 4096], P('tensor'), may hold values from -0.09375 to 0.09375
- post_gain: float32 [4096], replicated, may hold values from 0.25 to 1.75
- post_bias: float32 [4096], replicated, may hold values from -3 to 3
Outputs:
- block_out: bfloat16 [32768, 4096], P(('dp', 'tensor')), parts along dimension 0
There are 32 independent parts, one for each index of `dp`. A program takes and returns all parts, laid end to end along the dimension named above; an argument that names none is the same for every part. Nothing has to cross between parts.
Inputs may be any that keep to these rules, and one draw needn't show every extreme that they name: `segment_ids`: document numbers never fall along the stretch; every number appears; a document spans at most 512 tokens, and one exactly that many.
All inputs are finite; a program needn't handle non-finite values.
Results may differ from a plain program's by a relative error of at most 0.0065.
Values may be sent and summed in bfloat16 or wider, within the bound.
A program may use at most 128 MiB of HBM per device.

v0:
```python
import jax
import jax.numpy as jnp
from jax import lax
from jax.sharding import PartitionSpec as P

HEADS = 32
HEAD_DIM = 128


deep_alpha = 160.0**0.25


def body(
    queries,
    keys,
    values,
    segment_ids,
    residual,
    sub_gain,
    sub_bias,
    out_weight,
    post_gain,
    post_bias,
):
    q_heads, k_heads, v_heads = (
        lax.all_to_all(queries, "tensor", split_axis=1, concat_axis=0, tiled=True),
        lax.all_to_all(keys, "tensor", split_axis=1, concat_axis=0, tiled=True),
        lax.all_to_all(values, "tensor", split_axis=1, concat_axis=0, tiled=True),
    )
    count = q_heads.shape[0]
    local_heads = q_heads.shape[1] // HEAD_DIM
    q_split = q_heads.reshape(count, local_heads, HEAD_DIM)
    k_split = k_heads.reshape(count, local_heads, HEAD_DIM)
    v_split = v_heads.reshape(count, local_heads, HEAD_DIM)
    position = jnp.arange(count)
    allowed = (segment_ids[:, None] == segment_ids[None, :]) & (
        position[None, :] <= position[:, None]
    )
    scores = jnp.einsum("qhd,khd->hqk", q_split, k_split, preferred_element_type=jnp.float32) * (
        1.0 / HEAD_DIM**0.5
    )
    scores = jnp.where(allowed[None], scores, -jnp.inf)
    top = jnp.max(scores, axis=-1, keepdims=True)
    expo = jnp.exp(scores - top)
    probs = (expo / jnp.sum(expo, axis=-1, keepdims=True)).astype(jnp.bfloat16)
    attended = jnp.einsum(
        "hqk,khd->qhd", probs, v_split, preferred_element_type=jnp.float32
    ).reshape(count, local_heads * HEAD_DIM)
    inner = HEADS * HEAD_DIM
    total = lax.psum(jnp.sum(attended, axis=-1), "tensor")
    center = attended - (total / inner)[:, None]
    var = lax.psum(jnp.sum(center * center, axis=-1), "tensor") / inner
    normed = (center * lax.rsqrt(var[:, None] + 1e-05) * sub_gain + sub_bias).astype(jnp.bfloat16)
    projected = lax.psum_scatter(
        jnp.dot(normed, out_weight, preferred_element_type=jnp.float32).astype(jnp.bfloat16),
        "tensor",
        scatter_dimension=0,
        tiled=True,
    ).astype(jnp.float32)
    mixed = deep_alpha * residual.astype(jnp.float32) + projected
    centered = mixed - jnp.mean(mixed, axis=-1, keepdims=True)
    spread = jnp.mean(centered * centered, axis=-1, keepdims=True)
    return (centered * lax.rsqrt(spread + 1e-05) * post_gain + post_bias).astype(jnp.bfloat16)


def solution(mesh):
    return jax.shard_map(
        body,
        mesh=mesh,
        in_specs=(
            P(("dp", "tensor"), None),
            P(("dp", "tensor"), None),
            P(("dp", "tensor"), None),
            P("dp"),
            P(("dp", "tensor"), None),
            P("tensor"),
            P("tensor"),
            P("tensor", None),
            P(),
            P(),
        ),
        out_specs=P(("dp", "tensor"), None),
        check_vma=False,
    )
```

profile of v0, /device:TPU:32, one launch (start us, length us, event | category | flops | bytes accessed | tf_op | source)
XLA Modules:
  0.0 312.9 jit_solution(9259778366821469773)
XLA Ops:
  6.5 2.3 copy.19
  8.9 5.4 %all-to-all-start = ((bf16[128,8,512]{0,2,1:T(8,128)(2,1)}), bf16[128,8,512]{0,2,1:T(8,128)(2,1)S(1)}, u32[]{:S(2)}, u32[]{:S(2)}) async-start(bf16[128,8,512]{0,2,1:T(8,128)(2,1)} %bitcast), calls=%async_computation | async-start | bytes 2097152 | tf_op jit(solution)/shard_map/all_to_all | solution.py:26
  14.3 1.3 copy.21
  15.6 14.4 %all-to-all-done = bf16[128,8,512]{0,2,1:T(8,128)(2,1)S(1)} async-done(((bf16[128,8,512]{0,2,1:T(8,128)(2,1)}), bf16[128,8,512]{0,2,1:T(8,128)(2,1)S(1)}, u32[]{:S(2)}, u32[]{:S(2)}) %all-to-all-start) | async-done | bytes 1048608 | tf_op jit(solution)/shard_map/all_to_all | solution.py:26
  30.0 3.6 %all-to-all-start.1 = ((bf16[128,8,512]{0,2,1:T(8,128)(2,1)}), bf16[128,8,512]{0,2,1:T(8,128)(2,1)S(1)}, u32[]{:S(2)}, u32[]{:S(2)}) async-start(bf16[128,8,512]{0,2,1:T(8,128)(2,1)} %bitcast.2), calls=%async_computation.1 | async-start | bytes 2097152 | tf_op jit(solution)/shard_map/all_to_all | solution.py:27
  33.6 1.3 copy.25
  34.9 13.7 %all-to-all-done.1 = bf16[128,8,512]{0,2,1:T(8,128)(2,1)S(1)} async-done(((bf16[128,8,512]{0,2,1:T(8,128)(2,1)}), bf16[128,8,512]{0,2,1:T(8,128)(2,1)S(1)}, u32[]{:S(2)}, u32[]{:S(2)}) %all-to-all-start.1) | async-done | bytes 1048608 | tf_op jit(solution)/shard_map/all_to_all | solution.py:27
  48.6 3.6 %all-to-all-start.2 = ((bf16[128,8,512]{0,2,1:T(8,128)(2,1)}), bf16[128,8,512]{0,2,1:T(8,128)(2,1)S(1)}, u32[]{:S(2)}, u32[]{:S(2)}) async-start(bf16[128,8,512]{0,2,1:T(8,128)(2,1)} %bitcast.4), calls=%async_computation.2 | async-start | bytes 2097152 | tf_op jit(solution)/shard_map/all_to_all | solution.py:28
  52.2 1.6 fusion.6
  53.8 1.7 copy.20
  55.5 2.3 reshape.90
  57.8 0.7 copy.22
  58.5 1.3 reshape.91
  59.8 7.0 %all-to-all-done.2 = bf16[128,8,512]{0,2,1:T(8,128)(2,1)S(1)} async-done(((bf16[128,8,512]{0,2,1:T(8,128)(2,1)}), bf16[128,8,512]{0,2,1:T(8,128)(2,1)S(1)}, u32[]{:S(2)}, u32[]{:S(2)}) %all-to-all-start.2) | async-done | bytes 1048608 | tf_op jit(solution)/shard_map/all_to_all | solution.py:28
  66.7 0.7 copy.26
  67.4 1.3 reshape.92
  68.8 10.9 %fusion.18 = (f32[4,1024]{1,0:T(4,128)S(1)}, f32[4,1024,1024]{1,2,0:T(8,128)}) fusion(pred[1024,1024]{0,1:T(8,128)(4,1)S(1)} %copy-done.4, bf16[1024,4,128]{0,2,1:T(8,128)(2,1)S(1)} %copy-done.5, bf16[1024,4,128]{0,2,1:T(8,128)(2,1)} %reshape.91), kind=kOutput, calls=%fused_computation.31 | convolution fusion | flops 1090520064 | bytes 19939328 | tf_op jit(solution)/shard_map/sub | solution.py:44
  79.7 6.9 %fusion.19 = (f32[1024]{0:T(1024)S(1)}, f32[4,1024,128]{1,2,0:T(8,128)S(1)}) fusion(bf16[1024,4,128]{0,2,1:T(8,128)(2,1)} %reshape.92, f32[4,1024,1024]{1,2,0:T(8,128)} %get-tuple-element.6, f32[4,1024]{1,0:T(4,128)S(1)} %get-tuple-element.5), kind=kOutput, calls=%fused_computation.32 | convolution fusion | flops 1082653696 | bytes 19943424 | tf_op jit(solution)/shard_map/hqk,khd->qhd/dot_general | solution.py:46
  86.6 17.5 %psum.14 = f32[1024]{0:T(1024)S(1)} all-reduce(f32[1024]{0:T(1024)S(1)} %get-tuple-element.7), channel_id=1, replica_groups=mesh['dp'=32,'tensor'=8] {'tensor'}, use_global_device_ids=true, to_apply=%region_3.4 | all-reduce | flops 1024 | bytes 8192 | tf_op jit(solution)/shard_map/psum | solution.py:50
  104.5 16.7 %psum.15 = f32[1024]{0:T(1024)S(1)} all-reduce(f32[1024]{0:T(1024)S(1)} %fusion.12), channel_id=1, replica_groups=mesh['dp'=32,'tensor'=8] {'tensor'}, use_global_device_ids=true, to_apply=%region_5.6 | all-reduce | flops 1024 | bytes 8192 | tf_op jit(solution)/shard_map/psum | solution.py:52
  121.6 9.0 %convolution_convert_fusion = bf16[1024,4096]{1,0:T(8,128)(2,1)} fusion(bf16[1024,512]{0,1:T(8,128)(2,1)S(1)} %fusion.10, bf16[512,4096]{1,0:T(8,128)(2,1)} %param.17), kind=kOutput, calls=%fused_computation.9 | convolution fusion | flops 4299161600 | bytes 13631488 | tf_op jit(solution)/shard_map/dot_general | solution.py:55
  130.6 171.5 %reduce-scatter.2.cloned.1.call-done = bf16[128,4096]{1,0:T(8,128)(2,1)} async-done(((bf16[1024,4096]{1,0:T(8,128)(2,1)}), bf16[128,4096]{1,0:T(8,128)(2,1)}) %reduce-scatter.2.cloned.1.call-update) | async-done | bytes 1048592 | tf_op jit(solution)/shard_map/reduce_scatter | solution.py:54
  302.1 1.7 fusion.15
  304.5 1.6 add_convert_fusion
  (31 shorter events, 1.5 us)
Async XLA Ops:
  6.5 7.7 %copy-start.2 = (bf16[128,4096]{1,0:T(8,128)(2,1)S(1)}, bf16[128,4096]{1,0:T(8,128)(2,1)}, u32[]{:S(2)}) copy-start(bf16[128,4096]{1,0:T(8,128)(2,1)} %param.11) | copy-start | bytes 3145732
  8.9 21.1 %all-to-all-start = ((bf16[128,8,512]{0,2,1:T(8,128)(2,1)}), bf16[128,8,512]{0,2,1:T(8,128)(2,1)S(1)}, u32[]{:S(2)}, u32[]{:S(2)}) async-start(bf16[128,8,512]{0,2,1:T(8,128)(2,1)} %bitcast), calls=%async_computation | async-start | bytes 2097152 | tf_op jit(solution)/shard_map/all_to_all | solution.py:26
  14.3 19.3 %copy-start.3 = (bf16[128,4096]{1,0:T(8,128)(2,1)S(1)}, bf16[128,4096]{1,0:T(8,128)(2,1)}, u32[]{:S(2)}) copy-start(bf16[128,4096]{1,0:T(8,128)(2,1)} %param.12) | copy-start | bytes 3145732
  30.0 18.6 %all-to-all-start.1 = ((bf16[128,8,512]{0,2,1:T(8,128)(2,1)}), bf16[128,8,512]{0,2,1:T(8,128)(2,1)S(1)}, u32[]{:S(2)}, u32[]{:S(2)}) async-start(bf16[128,8,512]{0,2,1:T(8,128)(2,1)} %bitcast.2), calls=%async_computation.1 | async-start | bytes 2097152 | tf_op jit(solution)/shard_map/all_to_all | solution.py:27
  33.6 18.7 %copy-start.8 = (s32[1024]{0:T(1024)S(1)}, s32[1024]{0:T(1024)}, u32[]{:S(2)}) copy-start(s32[1024]{0:T(1024)} %param.13) | copy-start | bytes 12292
  48.6 18.1 %all-to-all-start.2 = ((bf16[128,8,512]{0,2,1:T(8,128)(2,1)}), bf16[128,8,512]{0,2,1:T(8,128)(2,1)S(1)}, u32[]{:S(2)}, u32[]{:S(2)}) async-start(bf16[128,8,512]{0,2,1:T(8,128)(2,1)} %bitcast.4), calls=%async_computation.2 | async-start | bytes 2097152 | tf_op jit(solution)/shard_map/all_to_all | solution.py:28
  52.2 250.0 %reduce-scatter.2.cloned.1.call-start = ((), (), s32[]{:S(2)}) async-start(), calls=%async_computation.4 | async-start | bytes 9437184 | tf_op jit(solution)/shard_map/reduce_scatter | solution.py:54
  66.7 2.0 copy-start.4
  67.4 1.4 copy-start.5
  86.6 34.6 %copy-start.9 = (f32[512]{0:T(512)S(1)}, f32[512]{0:T(512)}, u32[]{:S(2)}) copy-start(f32[512]{0:T(512)} %param.16) | copy-start | bytes 6148
  86.6 34.6 %copy-start.10 = (f32[512]{0:T(512)S(1)}, f32[512]{0:T(512)}, u32[]{:S(2)}) copy-start(f32[512]{0:T(512)} %param.15) | copy-start | bytes 6148
  130.5 171.6 %copy-start = (bf16[128,4096]{1,0:T(8,128)(2,1)S(1)}, bf16[128,4096]{1,0:T(8,128)(2,1)}, u32[]{:S(2)}) copy-start(bf16[128,4096]{1,0:T(8,128)(2,1)} %param.14) | copy-start | bytes 3145732
  130.6 173.9 %copy-start.6 = (f32[4096]{0:T(1024)S(1)}, f32[4096]{0:T(1024)}, u32[]{:S(2)}) copy-start(f32[4096]{0:T(1024)} %param.19) | copy-start | bytes 49156
  130.6 173.9 %copy-start.7 = (f32[4096]{0:T(1024)S(1)}, f32[4096]{0:T(1024)}, u32[]{:S(2)}) copy-start(f32[4096]{0:T(1024)} %param.18) | copy-start | bytes 49156
  302.1 1.7 copy-start.1
Sparse Core Ops, SparseCore 0:
  130.7 171.3 reduce-scatter.1
where the time goes:
time: 315 us; the launch traced here: 313 us
  waiting for transfers between devices  207 us (66%)
  blocking collectives  34.3 us (11%)
  matrix products  26.7 us (8%)
  between operations  13.6 us (4%)
  local copies, waits for them, and re-layouts  13.1 us (4%)
  starting transfers between devices  12.6 us (4%)
  other arithmetic  6.12 us (2%)
    reduce_scatter x1, waiting for transfers between devices, body(): lax.psum_scatter(jnp.dot(normed, out_weight, preferred_element_type=jnp.f...  172 us
    psum x1, blocking collectives, body(): total = lax.psum(jnp.sum(attended, axis=-1), 'tensor')  17.5 us
    psum x1, blocking collectives, body(): var = lax.psum(jnp.sum(center * center, axis=-1), 'tensor') / inner  16.7 us
    all_to_all x1, waiting for transfers between devices, body(): lax.all_to_all(queries, 'tensor', split_axis=1, concat_axis=0, tiled=True)  14.4 us
    all_to_all x1, waiting for transfers between devices, body(): lax.all_to_all(keys, 'tensor', split_axis=1, concat_axis=0, tiled=True)  13.7 us
    sub x1, matrix products, body(): expo = jnp.exp(scores - top)  10.9 us
    dot_general x1, matrix products, body(): jnp.dot(normed, out_weight, preferred_element_type=jnp.float32)  8.95 us
    all_to_all x1, waiting for transfers between devices, body(): lax.all_to_all(values, 'tensor', split_axis=1, concat_axis=0, tiled=True)  6.96 us
  transfers between devices with their start and end apart: 4, of which 4 were waited for; matrix products, arithmetic and copies ran while one was open for 3% of the time, Pallas kernels for 0%

commit v1 on v0

v1 whole, which is shorter than its diff:
```python
import functools

import jax
import jax.numpy as jnp
from jax import lax
from jax.experimental import pallas as pl
from jax.experimental.pallas import tpu as pltpu
from jax.sharding import PartitionSpec as P

HEAD_DIM = 128
TILE = 128
D = 4096
NY = 4
FEAT = 1024
NC = 4
CW = FEAT // NC
HPC = CW // HEAD_DIM
WCH = 4
WROWS = 256 // WCH
JC = 4
COL = 2048 // JC
WINDOW = (2, 4, 5, 5)
MESH = pl.DeviceIdType.MESH

deep_alpha = 160.0**0.25
LOG2E = 1.4426950408889634
SCALE = LOG2E / HEAD_DIM**0.5


def kernel(
    q, k, v, seg, res, gain, bias, w, pg, pb,
    out,
    qb, kb, vb, wb, gb, bb, mask, att, normed, stat, pbuf,
    oppb, rel, held, outb, fin, mixed, resb, pgb, pbb,
    loc_sem, y_send, y_recv, x_send, x_recv, w_send, w_recv, c_send, c_recv,
    g_send, g_recv, s_send, s_recv, o_send, o_recv, f_send, f_recv,
):
    dp = lax.axis_index("dp")
    t = lax.axis_index("tensor")
    core, hi, z = dp % 2, (dp // 2) % 2, dp // 4
    x, y = t % 2, t // 2

    def y_dev(d):
        return {"dp": dp, "tensor": ((y + d) % NY) * 2 + x}

    x_dev = {"dp": dp, "tensor": y * 2 + (1 - x)}
    wrap_dev = {"dp": z * 4 + (1 - hi) * 2 + core, "tensor": y * 2 + (1 - x)}
    core_dev = {"dp": z * 4 + hi * 2 + (1 - core), "tensor": t}

    def remote(src, dst, ss, rs, dev):
        return pltpu.make_async_remote_copy(
            src_ref=src, dst_ref=dst, send_sem=ss, recv_sem=rs, device_id=dev, device_id_type=MESH
        )

    def tile_rows(ty):
        return pl.ds(pl.multiple_of((2 * ty + x) * TILE, TILE), TILE)

    def cols(ty, c):
        return pl.ds(pl.multiple_of(ty * FEAT + c * CW, CW), CW)

    def y_copy(d, c, a):
        src = (q, k, v)[a].at[:, cols((y + d) % NY, c)]
        if a == 0:
            dst = qb.at[c, pl.ds(pl.multiple_of(y * TILE, TILE), TILE)]
        else:
            dst = (kb, vb)[a - 1].at[c, tile_rows(y)]
        return remote(src, dst, y_send.at[d - 1, c, a], y_recv.at[d - 1, c, a], y_dev(d))

    def x_copy(d, c, a):
        rows = tile_rows((y - d + NY) % NY)
        dst = (kb, vb)[a].at[c, rows]
        src = (k, v)[a].at[:, cols(y, c)] if d == 0 else dst
        return remote(src, dst, x_send.at[d, c, a], x_recv.at[d, c, a], x_dev)

    def x_recv_copy(d, c, a):
        ty = (y - d + NY) % NY
        rows = pl.ds(pl.multiple_of((2 * ty + 1 - x) * TILE, TILE), TILE)
        dst = (kb, vb)[a].at[c, rows]
        return remote(dst, dst, x_send.at[d, c, a], x_recv.at[d, c, a], x_dev)

    def y_recv_copy(d, c, a):
        ty = (y - d + NY) % NY
        if a == 0:
            dst = qb.at[c, pl.ds(pl.multiple_of(ty * TILE, TILE), TILE)]
        else:
            dst = (kb, vb)[a - 1].at[c, tile_rows(ty)]
        return remote(dst, dst, y_send.at[d - 1, c, a], y_recv.at[d - 1, c, a], y_dev(d))

    def own_copy(c, a):
        src = (q, k, v)[a].at[:, cols(y, c)]
        if a == 0:
            dst = qb.at[c, pl.ds(pl.multiple_of(y * TILE, TILE), TILE)]
        else:
            dst = (kb, vb)[a - 1].at[c, tile_rows(y)]
        return pltpu.make_async_copy(src, dst, loc_sem.at[c * 3 + a])

    def w_rows(owner, n, of_core):
        return pl.ds(pl.multiple_of(owner * 512 + of_core * 256 + n * WROWS, WROWS), WROWS)

    def w_copy(n):
        src = w.at[pl.ds(pl.multiple_of(core * 256 + n * WROWS, WROWS), WROWS)]
        return remote(src, wb.at[w_rows(x, n, core)], w_send.at[n], w_recv.at[n], wrap_dev)

    def w_recv_copy(n):
        dst = wb.at[w_rows(1 - x, n, core)]
        return remote(dst, dst, w_send.at[n], w_recv.at[n], wrap_dev)

    def c_copy(n):
        src = wb.at[w_rows(1 - x, n, core)]
        return remote(src, src, c_send.at[n], c_recv.at[n], core_dev)

    def c_recv_copy(n):
        dst = wb.at[w_rows(1 - x, n, 1 - core)]
        return remote(dst, dst, c_send.at[n], c_recv.at[n], core_dev)

    def g_copy(i):
        return remote((gain, bias)[i], (gb, bb)[i].at[x], g_send.at[i], g_recv.at[i], wrap_dev)

    def g_recv_copy(i):
        dst = (gb, bb)[i].at[1 - x]
        return remote(dst, dst, g_send.at[i], g_recv.at[i], wrap_dev)

    local = [own_copy(c, a) for c in range(NC) for a in range(3)]
    base = NC * 3
    local.append(
        pltpu.make_async_copy(
            w, wb.at[pl.ds(pl.multiple_of(x * 512, 512), 512)], loc_sem.at[base]
        )
    )
    local.append(pltpu.make_async_copy(gain, gb.at[x], loc_sem.at[base + 1]))
    local.append(pltpu.make_async_copy(bias, bb.at[x], loc_sem.at[base + 2]))
    local.append(pltpu.make_async_copy(res, resb, loc_sem.at[base + 3]))
    local.append(pltpu.make_async_copy(pg, pgb, loc_sem.at[base + 4]))
    local.append(pltpu.make_async_copy(pb, pbb, loc_sem.at[base + 5]))

    barrier = pltpu.get_barrier_semaphore()
    peers = [y_dev(1), y_dev(2), y_dev(3), x_dev, wrap_dev, core_dev]
    for dev in peers:
        pl.semaphore_signal(barrier, inc=1, device_id=dev, device_id_type=MESH)
    pl.semaphore_wait(barrier, len(peers))

    def send_first(c, carry):
        for d in (1, 3, 2):
            for a in (1, 2, 0):
                y_copy(d, c, a).start()
        for a in range(2):
            x_copy(0, c, a).start()
        w_copy(c).start()
        return carry

    lax.fori_loop(0, NC, send_first, 0)
    for i in range(2):
        g_copy(i).start()
    for copy in local:
        copy.start()

    for qi in range(NY):
        tq = 2 * qi + x
        first = (0, 0, x, 2 + x)[qi]
        row = seg[pl.ds(tq, 1), :].astype(jnp.float32)
        of_query = jnp.broadcast_to(row, (TILE, TILE)).T
        sub = lax.broadcasted_iota(jnp.int32, (TILE, TILE), 0) + tq * TILE
        lane = lax.broadcasted_iota(jnp.int32, (TILE, TILE), 1)
        for n in range(WINDOW[qi]):
            of_key = seg[pl.ds(first + n, 1), :].astype(jnp.float32)
            seen = (of_query == of_key) & (lane + (first + n) * TILE <= sub)
            mask[qi, :, n * TILE : (n + 1) * TILE] = jnp.where(seen, 0.0, -1e30)

    for copy in local:
        copy.wait()

    def receive_y(c):
        for d in (1, 3, 2):
            for a in (1, 2, 0):
                y_recv_copy(d, c, a).wait_recv()
        for d in (1, 3, 2):
            for a in range(2):
                x_copy(d, c, a).start()

    def attend(c):
        for d in range(NY):
            for a in range(2):
                x_recv_copy(d, c, a).wait_recv()
        for h in range(HPC):
            hc = pl.ds(h * HEAD_DIM, HEAD_DIM)
            for qi in range(NY):
                n = WINDOW[qi] * TILE
                first = (0, 0, x, 2 + x)[qi]
                keys = pl.ds(pl.multiple_of(first * TILE, TILE), n)
                rows = pl.ds(qi * TILE, TILE)
                s = lax.dot_general(
                    qb[c, rows, hc], kb[c, keys, hc], (((1,), (1,)), ((), ())),
                    preferred_element_type=jnp.float32,
                )
                s = s + mask[qi, :, :n]
                top = jnp.max(s, axis=-1, keepdims=True)
                p = jnp.exp2((s - top) * SCALE)
                total = jnp.sum(p, axis=-1, keepdims=True)
                o = jnp.dot(
                    p.astype(jnp.bfloat16), vb[c, keys, hc], preferred_element_type=jnp.float32
                )
                att[c, rows, hc] = o / total

    def forward_w(n):
        w_recv_copy(n).wait_recv()
        c_copy(n).start()

    receive_y(0)

    def chunk_step(c, carry):
        receive_y(c)
        forward_w(c - 1)
        attend(c - 1)
        return carry

    lax.fori_loop(1, NC, chunk_step, 0)
    forward_w(WCH - 1)
    attend(NC - 1)

    pad = lax.broadcasted_iota(jnp.int32, (TILE, TILE), 1)
    for qi in range(NY):
        rows = pl.ds(qi * TILE, TILE)
        mean = sum(jnp.sum(att[c, rows, :], axis=-1, keepdims=True) for c in range(NC)) / FEAT
        spread = sum(
            jnp.sum((att[c, rows, :] - mean) ** 2, axis=-1, keepdims=True) for c in range(NC)
        )
        both = jnp.where(pad == 0, mean, spread).T
        stat[0, qi] = both[:8]

    def s_copy(d):
        return remote(stat.at[0], stat.at[d], s_send.at[d - 1], s_recv.at[d - 1], y_dev(d))

    for d in (1, 2, 3):
        s_copy(d).start()
    for i in range(2):
        g_recv_copy(i).wait_recv()
    for d in (1, 2, 3):
        s_copy(d).wait_recv()
    for qi in range(NY):
        rows = pl.ds(qi * TILE, TILE)
        means = [stat[d, qi, 0:1, :] for d in range(NY)]
        mean = sum(means) / NY
        spread = sum(stat[d, qi, 1:2, :] for d in range(NY))
        spread = spread + FEAT * sum((m - mean) ** 2 for m in means)
        inv = lax.rsqrt(spread / (NY * FEAT) + 1e-05)
        sub = lax.broadcasted_iota(jnp.int32, (TILE, TILE), 0)
        both = jnp.where(sub == 0, mean, inv).T
        mean, inv = both[:, 0:1], both[:, 1:2]
        for c in range(NC):
            half = c * CW // 512
            lanes = pl.ds(c * CW % 512, CW)
            value = (att[c, rows, :] - mean) * inv * gb[half, :, lanes] + bb[half, :, lanes]
            normed[rows, c * CW : (c + 1) * CW] = value.astype(jnp.bfloat16)

    for n in range(WCH):
        c_recv_copy(n).wait_recv()

    def o_copy(half, j):
        return remote(
            oppb.at[half, j], rel.at[half, j], o_send.at[half, j], o_recv.at[half, j],
            y_dev(1 if half == 0 else 3),
        )

    def f_copy(way, half, j):
        return remote(
            outb.at[way, half, j], fin.at[way, half, j], f_send.at[way, half, j],
            f_recv.at[way, half, j], y_dev(1 if way == 0 else 3),
        )

    def rows_of(d):
        return pl.ds(pl.multiple_of(((y + d) % NY) * TILE, TILE), TILE)

    def project(j, carry):
        for half in range(2):
            col = pl.ds(pl.multiple_of(half * 2048 + j * COL, COL), COL)
            pbuf[...] = jnp.dot(normed[...], wb[:, col], preferred_element_type=jnp.float32)
            oppb[half, j] = pbuf[rows_of(2), :].astype(jnp.bfloat16)
            o_copy(half, j).start()
            way = 1 - half
            outb[way, half, j] = pbuf[rows_of(1 if way == 0 else 3), :].astype(jnp.bfloat16)
            f_copy(way, half, j).start()
            held[half, j] = pbuf[rows_of(1 if half == 0 else 3), :]
            mixed[half, j] = pbuf[rows_of(0), :] + deep_alpha * resb[:, col].astype(jnp.float32)
        return carry

    lax.fori_loop(0, JC, project, 0)

    def pass_on(j, carry):
        for half in range(2):
            o_copy(half, j).wait_recv()
            value = held[half, j] + rel[half, j].astype(jnp.float32)
            outb[half, half, j] = value.astype(jnp.bfloat16)
            f_copy(half, half, j).start()
        return carry

    lax.fori_loop(0, JC, pass_on, 0)

    def collect(j, total):
        for half in range(2):
            for way in range(2):
                f_copy(way, half, j).wait_recv()
            value = mixed[half, j] + fin[0, half, j].astype(jnp.float32)
            value = value + fin[1, half, j].astype(jnp.float32)
            mixed[half, j] = value
            total = total + jnp.sum(value, axis=-1, keepdims=True)
        return total

    total = lax.fori_loop(0, JC, collect, jnp.zeros((TILE, 1), jnp.float32))
    mean = total / D
    spread = jnp.zeros((TILE, 1), jnp.float32)
    for half in range(2):
        for j in range(JC):
            spread = spread + jnp.sum((mixed[half, j] - mean) ** 2, axis=-1, keepdims=True)
    inv = lax.rsqrt(spread / D + 1e-05)
    for half in range(2):
        for j in range(JC):
            col = pl.ds(half * 2048 + j * COL, COL)
            value = (mixed[half, j] - mean) * inv * pgb[:, col] + pbb[:, col]
            out[:, col] = value.astype(jnp.bfloat16)

    def sent(c, carry):
        for d in (1, 3, 2):
            for a in range(3):
                y_copy(d, c, a).wait_send()
        for d in range(NY):
            for a in range(2):
                x_copy(d, c, a).wait_send()
        w_copy(c).wait_send()
        c_copy(c).wait_send()
        return carry

    lax.fori_loop(0, NC, sent, 0)
    for i in range(2):
        g_copy(i).wait_send()
    for d in (1, 2, 3):
        s_copy(d).wait_send()

    def sent_shares(j, carry):
        for half in range(2):
            o_copy(half, j).wait_send()
            for way in range(2):
                f_copy(way, half, j).wait_send()
        return carry

    lax.fori_loop(0, JC, sent_shares, 0)


def body(
    queries, keys, values, segment_ids, residual, sub_gain, sub_bias, out_weight, post_gain, post_bias
):
    any_spec = pl.BlockSpec(memory_space=pl.ANY)
    vmem_spec = pl.BlockSpec(memory_space=pltpu.VMEM)
    bf16, f32 = jnp.bfloat16, jnp.float32
    dma = pltpu.SemaphoreType.DMA
    return pl.pallas_call(
        kernel,
        name="block",
        out_shape=jax.ShapeDtypeStruct((TILE, D), bf16),
        in_specs=[any_spec] * 3 + [vmem_spec] + [any_spec] * 6,
        out_specs=vmem_spec,
        scratch_shapes=[
            pltpu.VMEM((NC, NY * TILE, CW), bf16),
            pltpu.VMEM((NC, 8 * TILE, CW), bf16),
            pltpu.VMEM((NC, 8 * TILE, CW), bf16),
            pltpu.VMEM((FEAT, D), bf16),
            pltpu.VMEM((2, 1, 512), f32),
            pltpu.VMEM((2, 1, 512), f32),
            pltpu.VMEM((NY, TILE, 5 * TILE), f32),
            pltpu.VMEM((NC, NY * TILE, CW), f32),
            pltpu.VMEM((NY * TILE, FEAT), bf16),
            pltpu.VMEM((NY, NY, 8, TILE), f32),
            pltpu.VMEM((NY * TILE, COL), f32),
            pltpu.VMEM((2, JC, TILE, COL), bf16),
            pltpu.VMEM((2, JC, TILE, COL), bf16),
            pltpu.VMEM((2, JC, TILE, COL), f32),
            pltpu.VMEM((2, 2, JC, TILE, COL), bf16),
            pltpu.VMEM((2, 2, JC, TILE, COL), bf16),
            pltpu.VMEM((2, JC, TILE, COL), f32),
            pltpu.VMEM((TILE, D), bf16),
            pltpu.VMEM((1, D), f32),
            pltpu.VMEM((1, D), f32),
            dma((NC * 3 + 6,)),
            dma((3, NC, 3)),
            dma((3, NC, 3)),
            dma((NY, NC, 2)),
            dma((NY, NC, 2)),
            dma((WCH,)),
            dma((WCH,)),
            dma((WCH,)),
            dma((WCH,)),
            dma((2,)),
            dma((2,)),
            dma((3,)),
            dma((3,)),
            dma((2, JC)),
            dma((2, JC)),
            dma((2, 2, JC)),
            dma((2, 2, JC)),
        ],
        compiler_params=pltpu.CompilerParams(
            collective_id=0, has_side_effects=True, vmem_limit_bytes=56 << 20
        ),
    )(
        queries,
        keys,
        values,
        segment_ids.reshape(8, TILE),
        residual,
        sub_gain.reshape(1, 512),
        sub_bias.reshape(1, 512),
        out_weight,
        post_gain.reshape(1, D),
        post_bias.reshape(1, D),
    )


def solution(mesh):
    return jax.shard_map(
        body,
        mesh=mesh,
        in_specs=(
            P(("dp", "tensor"), None),
            P(("dp", "tensor"), None),
            P(("dp", "tensor"), None),
            P("dp"),
            P(("dp", "tensor"), None),
            P("tensor"),
            P("tensor"),
            P("tensor", None),
            P(),
            P(),
        ),
        out_specs=P(("dp", "tensor"), None),
        check_vma=False,
    )
```

time: 315 us -> 101 us (0.32)
  waiting for transfers between devices: 207 us -> 0 us
  Pallas kernels: 0 us -> 98.1 us
  blocking collectives: 34.3 us -> 0 us
  matrix products: 26.7 us -> 0 us
  between operations: 13.6 us -> 0.01 us
  starting transfers between devices: 12.6 us -> 0 us
  local copies, waits for them, and re-layouts: 13.1 us -> 2.29 us
  other arithmetic: 6.12 us -> 0 us
    reduce_scatter x1 -> x0, waiting for transfers between devices: 172 us -> none  [body(): lax.psum_scatter(jnp.dot(normed, out_weight, preferred_element_type=jnp.f...]
    pallas_call x0 -> x1, Pallas kernels: none -> 98.1 us  [body(): pl.pallas_call(kernel, name='block', out_shape=jax.ShapeDtypeStruct((TILE...]
    all_to_all x3 -> x0, waiting for transfers between devices: 35 us -> none  [the longest x1 14.4 us: body(): lax.all_to_all(queries, 'tensor', split_axis=1, concat_axis=0, tiled=True)]
    psum x2 -> x0, blocking collectives: 34.3 us -> none  [the longest x1 17.5 us: body(): total = lax.psum(jnp.sum(attended, axis=-1), 'tensor')]
    dot_general x2 -> x0, matrix products: 15.8 us -> none  [the longest x1 8.95 us: body(): jnp.dot(normed, out_weight, preferred_element_type=jnp.float32)]
    all_to_all x3 -> x0, starting transfers between devices: 12.5 us -> none  [the longest x1 5.4 us: body(): lax.all_to_all(queries, 'tensor', split_axis=1, concat_axis=0, tiled=True)]
    sub x1 -> x0, matrix products: 10.9 us -> none  [body(): expo = jnp.exp(scores - top)]
    reshape x3 -> x0, local copies, waits for them, and re-layouts: 4.87 us -> none  [the longest x1 2.31 us: body(): q_split = q_heads.reshape(count, local_heads, HEAD_DIM)]
  transfers between devices with their start and end apart: 4 -> 0, of which waited for: 4 -> 0; matrix products, arithmetic and copies ran while one was open for 3% -> 0% of each run, Pallas kernels for 0% -> 0%
where the time goes in v1:
time: 101 us; the launch traced here: 100 us
  Pallas kernels  98.1 us (97%)
  local copies, waits for them, and re-layouts  2.29 us (2%)
    pallas_call x1, Pallas kernels, body(): pl.pallas_call(kernel, name='block', out_shape=jax.ShapeDtypeStruct((TILE...  98.1 us
    unnamed x1, local copies, waits for them, and re-layouts  2.29 us

profile of v1, /device:TPU:32, one launch (start us, length us, event | category | flops | bytes accessed | tf_op | source)
XLA Modules:
  0.0 100.4 jit_solution(14045215170431402311)
XLA Ops:
  0.0 98.1 %block.1 = bf16[128,4096]{1,0:T(8,128)(2,1)} custom-call(bf16[128,4096]{1,0:T(8,128)(2,1)} %q.1, bf16[128,4096]{1,0:T(8,128)(2,1)} %k.1, bf16[128,4096]{1,0:T(8,128)(2,1)} %v.1, s32[8,128]{1,0:T(8,128)} %bitcast.7, bf16[128,4096]{1,0:T(8,128)(2,1)} %res.1, f32[1,512]{1,0:T(1,128)} %bitcast.8, f32[1,512]{1,0:T(1,128)} %bitcast.9, bf16[512,4096]{1,0:T(8,128)(2,1)} %w.1, ...), custom_call_target="tpu_custom_call" | custom-call | tf_op jit(solution)/shard_map/block/pallas_call | solution.py:355
  98.1 2.3 %copy.12 = bf16[128,4096]{1,0:T(8,128)(2,1)} copy(bf16[128,4096]{1,0:T(8,128)(2,1)} %block.1) | data formatting | bytes 2097152

commit v2 on v1

v2 whole, which is shorter than its diff:
```python
import jax
import jax.numpy as jnp
from jax import lax
from jax.experimental import pallas as pl
from jax.experimental.pallas import tpu as pltpu
from jax.sharding import PartitionSpec as P

HEAD_DIM = 128
TILE = 128
D = 4096
NY = 4
LATE = NY - 1
FEAT = 1024
NC = 8
CW = FEAT // NC
HPC = CW // HEAD_DIM
EARLY = 3 * NC // 8
WN = 4
WROWS = 128 // WN
JC = 4
COL = 2048 // JC
EXTRA = 16
ROWS = LATE * TILE + EXTRA
WINDOW = (2, 4, 5, 5)
MESH = pl.DeviceIdType.MESH

deep_alpha = 160.0**0.25
LOG2E = 1.4426950408889634
SCALE = LOG2E / HEAD_DIM**0.5


def kernel(
    q, k, v, seg, res, gain, bias, w, pg, pb,
    out,
    qb, kb, vb, wb, gb, bb, mask, att, left, left_late, stat, stat_in, vec, pbuf,
    oppb, rel, held, outb, fin, mixed, resb, pgb, pbb,
    loc_sem, y_send, y_recv, x_send, x_recv, w_send, w_recv, c_send, c_recv, z_send, z_recv,
    g_send, g_recv, s_send, s_recv, v_send, v_recv, o_send, o_recv, f_send, f_recv,
):
    dp = lax.axis_index("dp")
    t = lax.axis_index("tensor")
    core, hi, z = dp % 2, (dp // 2) % 2, dp // 4
    x, y = t % 2, t // 2
    zpar = z % 2

    def y_dev(ty):
        return {"dp": dp, "tensor": ty * 2 + x}

    x_dev = {"dp": dp, "tensor": y * 2 + (1 - x)}
    wrap_dev = {"dp": z * 4 + (1 - hi) * 2 + core, "tensor": y * 2 + (1 - x)}
    core_dev = {"dp": z * 4 + hi * 2 + (1 - core), "tensor": t}
    z_dev = {"dp": (z + 1 - 2 * zpar) * 4 + hi * 2 + core, "tensor": t}
    up, far, down = (y + 1) % NY, (y + 2) % NY, (y + 3) % NY

    def remote(src, dst, ss, rs, dev):
        return pltpu.make_async_remote_copy(
            src_ref=src, dst_ref=dst, send_sem=ss, recv_sem=rs, device_id=dev, device_id_type=MESH
        )

    def rows_at(n, size):
        return pl.ds(pl.multiple_of(n * size, size), size)

    def cols(ty, c):
        return pl.ds(pl.multiple_of(ty * FEAT + c * CW, CW), CW)

    def slot(a, ty, c):
        if a == 0:
            return qb.at[c, rows_at(ty, TILE)]
        return (kb, vb)[a - 1].at[c, rows_at(2 * ty + x, TILE)]

    def y_copy(n, c, a):
        ty = (y + n) % NY
        return remote(
            (q, k, v)[a].at[:, cols(ty, c)], slot(a, y, c),
            y_send.at[n - 1, c, a], y_recv.at[y, c, a], y_dev(ty),
        )

    def y_wait(ty, c, a):
        dst = slot(a, ty, c)
        remote(dst, dst, y_send.at[0, c, a], y_recv.at[ty, c, a], y_dev(ty)).wait_recv()

    def x_copy(ty, c, a):
        dst = slot(a, ty, c)
        return remote(dst, dst, x_send.at[ty, c, a - 1], x_recv.at[ty, c, a - 1], x_dev)

    def x_own(c, a):
        return remote(
            (q, k, v)[a].at[:, cols(y, c)], slot(a, y, c),
            x_send.at[y, c, a - 1], x_recv.at[y, c, a - 1], x_dev,
        )

    def x_wait(ty, c, a):
        dst = (kb, vb)[a - 1].at[c, rows_at(2 * ty + 1 - x, TILE)]
        remote(dst, dst, x_send.at[ty, c, a - 1], x_recv.at[ty, c, a - 1], x_dev).wait_recv()

    def piece(owner, of_core, of_z, n):
        return wb.at[rows_at(owner * 16 + of_core * 8 + of_z * 4 + n, WROWS)]

    def w_copy(n):
        src = w.at[rows_at(core * 8 + zpar * 4 + n, WROWS)]
        return remote(src, piece(x, core, zpar, n), w_send.at[n], w_recv.at[n], wrap_dev)

    def w_wait(n):
        dst = piece(1 - x, core, zpar, n)
        remote(dst, dst, w_send.at[n], w_recv.at[n], wrap_dev).wait_recv()

    def z_copy(n):
        src = piece(1 - x, core, zpar, n)
        return remote(src, src, z_send.at[n], z_recv.at[n], z_dev)

    def z_wait(n):
        dst = piece(1 - x, core, 1 - zpar, n)
        remote(dst, dst, z_send.at[n], z_recv.at[n], z_dev).wait_recv()

    def c_copy(of_z, n):
        src = piece(1 - x, core, of_z, n)
        return remote(src, src, c_send.at[of_z, n], c_recv.at[of_z, n], core_dev)

    def c_wait(of_z, n):
        dst = piece(1 - x, 1 - core, of_z, n)
        remote(dst, dst, c_send.at[of_z, n], c_recv.at[of_z, n], core_dev).wait_recv()

    def g_copy(i):
        return remote((gain, bias)[i], (gb, bb)[i].at[x], g_send.at[i], g_recv.at[i], wrap_dev)

    def g_wait(i):
        dst = (gb, bb)[i].at[1 - x]
        remote(dst, dst, g_send.at[i], g_recv.at[i], wrap_dev).wait_recv()

    def s_copy(ty):
        return remote(stat.at[ty], stat_in.at[y], s_send.at[ty], s_recv.at[y], y_dev(ty))

    def s_wait(ty):
        dst = stat_in.at[ty]
        remote(dst, dst, s_send.at[ty], s_recv.at[ty], y_dev(ty)).wait_recv()

    def v_copy(n):
        ty = (y + n) % NY
        return remote(vec.at[y], vec.at[y], v_send.at[n - 1], v_recv.at[y], y_dev(ty))

    def v_wait(ty):
        dst = vec.at[ty]
        remote(dst, dst, v_send.at[0], v_recv.at[ty], y_dev(ty)).wait_recv()

    def o_copy(half, j):
        return remote(
            oppb.at[half, j], rel.at[half, j], o_send.at[half, j], o_recv.at[half, j],
            y_dev((up, down)[half]),
        )

    def f_copy(way, half, j):
        return remote(
            outb.at[way, half, j], fin.at[way, half, j], f_send.at[way, half, j],
            f_recv.at[way, half, j], y_dev((up, down)[way]),
        )

    local = []

    def fetch(src, dst):
        local.append(pltpu.make_async_copy(src, dst, loc_sem.at[len(local)]))

    for c in range(NC):
        for a in range(3):
            fetch((q, k, v)[a].at[:, cols(y, c)], slot(a, y, c))
    fetch(gain, gb.at[x])
    fetch(bias, bb.at[x])
    fetch(pg, pgb)
    fetch(pb, pbb)
    fetch(res, resb)
    fetch(w, wb.at[rows_at(x, 512)])

    barrier = pltpu.get_barrier_semaphore()
    peers = [y_dev(up), y_dev(far), y_dev(down), x_dev, wrap_dev, core_dev, z_dev]
    for dev in peers:
        pl.semaphore_signal(barrier, inc=1, device_id=dev, device_id_type=MESH)
    pl.semaphore_wait(barrier, len(peers))

    def send_kv(c, carry):
        for n in (1, 3, 2):
            for a in (1, 2):
                y_copy(n, c, a).start()

        @pl.when((y != LATE) | ((x == 0) & (c < EARLY)))
        def _():
            for a in (1, 2):
                x_own(c, a).start()

        return carry

    def send_q(c, carry):
        for n in (1, 3, 2):
            y_copy(n, c, 0).start()
        return carry

    lax.fori_loop(0, 1, send_kv, 0)
    for n in range(WN):
        w_copy(n).start()
    lax.fori_loop(1, NC, send_kv, 0)
    for i in range(2):
        g_copy(i).start()
    lax.fori_loop(0, NC, send_q, 0)
    for copy in local:
        copy.start()

    first_of = (0, 0, x, 2 + x)
    for qi in range(NY):
        tq = 2 * qi + x
        row = seg[pl.ds(tq, 1), :].astype(jnp.float32)
        of_query = jnp.broadcast_to(row, (TILE, TILE)).T
        sub = lax.broadcasted_iota(jnp.int32, (TILE, TILE), 0) + tq * TILE
        lane = lax.broadcasted_iota(jnp.int32, (TILE, TILE), 1)
        for n in range(WINDOW[qi]):
            of_key = seg[pl.ds(first_of[qi] + n, 1), :].astype(jnp.float32)
            seen = (of_query == of_key) & (lane + (first_of[qi] + n) * TILE <= sub)
            mask[qi, :, n * TILE : (n + 1) * TILE] = jnp.where(seen, 0.0, -1e30)

    for copy in local:
        copy.wait()

    def receive_kv(c):
        for ty in range(NY):

            @pl.when(ty != y)
            def _():
                for a in (1, 2):
                    y_wait(ty, c, a)
                    if ty != LATE:
                        x_copy(ty, c, a).start()

    def spread_z(n):
        z_wait(n)
        c_copy(1 - zpar, n).start()

    def relay(i, carry):
        for h in range(NC // WN):
            receive_kv(i * (NC // WN) + h)
        w_wait(i)
        c_copy(zpar, i).start()
        z_copy(i).start()

        @pl.when(i >= 2)
        def _():
            spread_z(i - 2)

        return carry

    lax.fori_loop(0, WN, relay, 0)

    def relay_late(c, carry):
        @pl.when((x == 0) & ((y != LATE) | (c >= EARLY)))
        def _():
            for a in (1, 2):
                x_copy(LATE, c, a).start()

        return carry

    lax.fori_loop(0, NC, relay_late, 0)

    def attend(c, tiles):
        for h in range(HPC):
            hc = pl.ds(h * HEAD_DIM, HEAD_DIM)
            for qi in tiles:
                n = WINDOW[qi] * TILE
                keys = pl.ds(pl.multiple_of(first_of[qi] * TILE, TILE), n)
                rows = pl.ds(qi * TILE, TILE)
                s = lax.dot_general(
                    qb[c, rows, hc], kb[c, keys, hc], (((1,), (1,)), ((), ())),
                    preferred_element_type=jnp.float32,
                )
                s = s + mask[qi, :, :n]
                top = jnp.max(s, axis=-1, keepdims=True)
                p = jnp.exp2((s - top) * SCALE)
                total = jnp.sum(p, axis=-1, keepdims=True)
                o = jnp.dot(
                    p.astype(jnp.bfloat16), vb[c, keys, hc], preferred_element_type=jnp.float32
                )
                att[c, rows, hc] = o / total

    def first_tiles(c, carry):
        for ty in range(NY):

            @pl.when(ty != y)
            def _():
                y_wait(ty, c, 0)

        for ty in range(LATE):
            for a in (1, 2):
                x_wait(ty, c, a)
        attend(c, range(LATE))

        @pl.when((c == NC // 4) | (c == NC // 2))
        def _():
            spread_z(2 + (c * 4) // NC - 1)

        return carry

    lax.fori_loop(0, NC, first_tiles, 0)

    lane = lax.broadcasted_iota(jnp.int32, (TILE, TILE), 1)

    def lanes_of(c):
        return c * CW // 512, pl.ds(c * CW % 512, CW)

    def center(qi, dst, at):
        rows = pl.ds(qi * TILE, TILE)
        mean = sum(jnp.sum(att[c, rows, :], axis=-1, keepdims=True) for c in range(NC)) / FEAT
        spread = jnp.zeros((TILE, 1), jnp.float32)
        for c in range(NC):
            half, lanes = lanes_of(c)
            value = att[c, rows, :] - mean
            spread = spread + jnp.sum(value * value, axis=-1, keepdims=True)
            dst[at : at + TILE, c * CW : (c + 1) * CW] = (value * gb[half, :, lanes]).astype(
                jnp.bfloat16
            )
        stat[qi] = jnp.where(lane == 0, mean, spread).T[:8]

        @pl.when(qi != y)
        def _():
            s_copy(qi).start()

        @pl.when(qi == y)
        def _():
            stat_in[y] = stat[qi]

    for i in range(2):
        g_wait(i)
    sub = lax.broadcasted_iota(jnp.int32, (EXTRA, CW), 0)
    for c in range(NC):
        half, lanes = lanes_of(c)
        value = jnp.zeros((EXTRA, CW), jnp.float32)
        for i in range(2):
            row = (gb, bb)[i][half, :, lanes]
            high = row.astype(jnp.bfloat16).astype(jnp.float32)
            value = jnp.where(sub == 2 * i, high, jnp.where(sub == 2 * i + 1, row - high, value))
        left[LATE * TILE : ROWS, c * CW : (c + 1) * CW] = value.astype(jnp.bfloat16)
    for qi in range(LATE):
        center(qi, left, qi * TILE)

    for of_z in range(2):
        for n in range(WN):
            c_wait(of_z, n)

    def col(half, j):
        return pl.ds(pl.multiple_of(half * 2048 + j * COL, COL), COL)

    def hand_out(role, half, j, rows, start):
        value = pbuf[rows, :]
        if role == 2:
            oppb[half, j] = value.astype(jnp.bfloat16)
            o_copy(half, j).start()
        elif role == 0:
            mixed[half, j] = value
        else:
            way = 0 if role == 1 else 1
            if half == way:
                held[half, j] = value
            else:
                outb[way, half, j] = value.astype(jnp.bfloat16)
                if start:
                    f_copy(way, half, j).start()

    def project(j, carry):
        for half in range(2):
            pbuf[...] = jnp.dot(left[...], wb[:, col(half, j)], preferred_element_type=jnp.float32)
            for role in (2, 1, 3, 0):
                ty = (y + role) % NY

                @pl.when(ty != LATE)
                def _():
                    hand_out(role, half, j, rows_at(ty, TILE), False)

            extra = pbuf[LATE * TILE : ROWS, :]
            vec[y, 0, :, col(half, j)] = extra[0:1] + extra[1:2]
            vec[y, 1, :, col(half, j)] = extra[2:3] + extra[3:4]
        return carry

    lax.fori_loop(0, JC, project, 0)

    def send_direct(j, carry):
        @pl.when(up != LATE)
        def _():
            f_copy(0, 1, j).start()

        @pl.when(down != LATE)
        def _():
            f_copy(1, 0, j).start()

        return carry

    lax.fori_loop(0, JC, send_direct, 0)
    for n in (1, 3, 2):
        v_copy(n).start()

    def last_tile(c, carry):
        @pl.when(x == 1)
        def _():
            for a in (1, 2):
                x_wait(LATE, c, a)

        attend(c, (LATE,))
        return carry

    lax.fori_loop(0, NC, last_tile, 0)
    center(LATE, left_late, 0)

    def project_late(j, carry):
        for half in range(2):
            pbuf[:TILE] = jnp.dot(
                left_late[...], wb[:, col(half, j)], preferred_element_type=jnp.float32
            )
            for role in (2, 1, 3, 0):

                @pl.when((y + role) % NY == LATE)
                def _():
                    hand_out(role, half, j, pl.ds(0, TILE), True)

        return carry

    lax.fori_loop(0, JC, project_late, 0)

    def pass_on(half, j):
        o_copy(half, j).wait_recv()
        value = held[half, j] + rel[half, j].astype(jnp.float32)
        outb[half, half, j] = value.astype(jnp.bfloat16)
        f_copy(half, half, j).start()

    def pass_first(j, carry):
        for half in range(2):

            @pl.when((up, down)[half] != LATE)
            def _():
                pass_on(half, j)

        return carry

    def pass_late(j, carry):
        for half in range(2):

            @pl.when((up, down)[half] == LATE)
            def _():
                pass_on(half, j)

        return carry

    lax.fori_loop(0, JC, pass_first, 0)
    lax.fori_loop(0, JC, pass_late, 0)

    for ty in range(NY):

        @pl.when(ty != y)
        def _():
            s_wait(ty)
            v_wait(ty)

    means = [stat_in[ty, 0:1, :] for ty in range(NY)]
    mean = sum(means) / NY
    spread = sum(stat_in[ty, 1:2, :] for ty in range(NY))
    spread = spread + FEAT * sum((m - mean) ** 2 for m in means)
    inv = lax.rsqrt(spread / (NY * FEAT) + 1e-05)
    sub = lax.broadcasted_iota(jnp.int32, (TILE, TILE), 0)
    both = jnp.broadcast_to(inv, (TILE, TILE))
    for ty in range(NY):
        both = jnp.where(sub == ty, means[ty] - mean, both)
    both = both.T
    inv = both[:, NY : NY + 1]

    def prepare(j, carry):
        for half in range(2):
            value = mixed[half, j]
            shift = jnp.zeros((1, COL), jnp.float32)
            for ty in range(NY):
                value = value + both[:, ty : ty + 1] * vec[ty, 0, :, col(half, j)]
                shift = shift + vec[ty, 1, :, col(half, j)]
            stream = deep_alpha * resb[:, col(half, j)].astype(jnp.float32)
            mixed[half, j] = value * inv + shift + stream
        return carry

    lax.fori_loop(0, JC, prepare, 0)

    def collect(j, total):
        for half in range(2):
            for way in range(2):
                f_copy(way, half, j).wait_recv()
            value = fin[0, half, j].astype(jnp.float32) + fin[1, half, j].astype(jnp.float32)
            value = mixed[half, j] + inv * value
            mixed[half, j] = value
            total = total + jnp.sum(value, axis=-1, keepdims=True)
        return total

    total = lax.fori_loop(0, JC, collect, jnp.zeros((TILE, 1), jnp.float32))
    mean = total / D
    spread = jnp.zeros((TILE, 1), jnp.float32)
    for half in range(2):
        for j in range(JC):
            spread = spread + jnp.sum((mixed[half, j] - mean) ** 2, axis=-1, keepdims=True)
    inv = lax.rsqrt(spread / D + 1e-05)
    for half in range(2):
        for j in range(JC):
            lanes = pl.ds(half * 2048 + j * COL, COL)
            value = (mixed[half, j] - mean) * inv * pgb[:, lanes] + pbb[:, lanes]
            out[:, lanes] = value.astype(jnp.bfloat16)

    def sent(c, carry):
        for n in (1, 2, 3):
            for a in range(3):
                y_copy(n, c, a).wait_send()
        for ty in range(NY):

            @pl.when((ty != LATE) | (x == 0))
            def _():
                for a in (1, 2):
                    x_copy(ty, c, a).wait_send()

        return carry

    lax.fori_loop(0, NC, sent, 0)
    for n in range(WN):
        w_copy(n).wait_send()
        z_copy(n).wait_send()
        for of_z in range(2):
            c_copy(of_z, n).wait_send()
    for i in range(2):
        g_copy(i).wait_send()
    for ty in range(NY):

        @pl.when(ty != y)
        def _():
            s_copy(ty).wait_send()

    for n in (1, 2, 3):
        v_copy(n).wait_send()

    def sent_shares(j, carry):
        for half in range(2):
            o_copy(half, j).wait_send()
            for way in range(2):
                f_copy(way, half, j).wait_send()
        return carry

    lax.fori_loop(0, JC, sent_shares, 0)


def body(
    queries, keys, values, segment_ids, residual, sub_gain, sub_bias, out_weight, post_gain, post_bias
):
    any_spec = pl.BlockSpec(memory_space=pl.ANY)
    vmem_spec = pl.BlockSpec(memory_space=pltpu.VMEM)
    bf16, f32 = jnp.bfloat16, jnp.float32
    dma = pltpu.SemaphoreType.DMA
    return pl.pallas_call(
        kernel,
        name="block",
        out_shape=jax.ShapeDtypeStruct((TILE, D), bf16),
        in_specs=[any_spec] * 3 + [vmem_spec] + [any_spec] * 6,
        out_specs=vmem_spec,
        scratch_shapes=[
            pltpu.VMEM((NC, NY * TILE, CW), bf16),
            pltpu.VMEM((NC, 8 * TILE, CW), bf16),
            pltpu.VMEM((NC, 8 * TILE, CW), bf16),
            pltpu.VMEM((FEAT, D), bf16),
            pltpu.VMEM((2, 1, 512), f32),
            pltpu.VMEM((2, 1, 512), f32),
            pltpu.VMEM((NY, TILE, 5 * TILE), f32),
            pltpu.VMEM((NC, NY * TILE, CW), f32),
            pltpu.VMEM((ROWS, FEAT), bf16),
            pltpu.VMEM((TILE, FEAT), bf16),
            pltpu.VMEM((NY, 8, TILE), f32),
            pltpu.VMEM((NY, 8, TILE), f32),
            pltpu.VMEM((NY, 2, 1, D), f32),
            pltpu.VMEM((ROWS, COL), f32),
            pltpu.VMEM((2, JC, TILE, COL), bf16),
            pltpu.VMEM((2, JC, TILE, COL), bf16),
            pltpu.VMEM((2, JC, TILE, COL), f32),
            pltpu.VMEM((2, 2, JC, TILE, COL), bf16),
            pltpu.VMEM((2, 2, JC, TILE, COL), bf16),
            pltpu.VMEM((2, JC, TILE, COL), f32),
            pltpu.VMEM((TILE, D), bf16),
            pltpu.VMEM((1, D), f32),
            pltpu.VMEM((1, D), f32),
            dma((NC * 3 + 6,)),
            dma((3, NC, 3)),
            dma((NY, NC, 3)),
            dma((NY, NC, 2)),
            dma((NY, NC, 2)),
            dma((WN,)),
            dma((WN,)),
            dma((2, WN)),
            dma((2, WN)),
            dma((WN,)),
            dma((WN,)),
            dma((2,)),
            dma((2,)),
            dma((NY,)),
            dma((NY,)),
            dma((3,)),
            dma((NY,)),
            dma((2, JC)),
            dma((2, JC)),
            dma((2, 2, JC)),
            dma((2, 2, JC)),
        ],
        compiler_params=pltpu.CompilerParams(
            collective_id=0, has_side_effects=True, vmem_limit_bytes=56 << 20
        ),
    )(
        queries,
        keys,
        values,
        segment_ids.reshape(8, TILE),
        residual,
        sub_gain.reshape(1, 512),
        sub_bias.reshape(1, 512),
        out_weight,
        post_gain.reshape(1, D),
        post_bias.reshape(1, D),
    )


def solution(mesh):
    return jax.shard_map(
        body,
        mesh=mesh,
        in_specs=(
            P(("dp", "tensor"), None),
            P(("dp", "tensor"), None),
            P(("dp", "tensor"), None),
            P("dp"),
            P(("dp", "tensor"), None),
            P("tensor"),
            P("tensor"),
            P("tensor", None),
            P(),
            P(),
        ),
        out_specs=P(("dp", "tensor"), None),
        check_vma=False,
    )
```

time: 101 us -> 92.4 us (0.915)
  Pallas kernels: 98.1 us -> 89.9 us
    pallas_call x1, Pallas kernels: 98.1 us -> 89.9 us  [body(): pl.pallas_call(kernel, name='block', out_shape=jax.ShapeDtypeStruct((TILE...]
where the time goes in v2:
time: 92.4 us; the launch traced here: 92.2 us
  Pallas kernels  89.9 us (97%)
  local copies, waits for them, and re-layouts  2.29 us (2%)
    pallas_call x1, Pallas kernels, body(): pl.pallas_call(kernel, name='block', out_shape=jax.ShapeDtypeStruct((TILE...  89.9 us
    unnamed x1, local copies, waits for them, and re-layouts  2.29 us

profile of v2, /device:TPU:32, one launch (start us, length us, event | category | flops | bytes accessed | tf_op | source)
XLA Modules:
  0.0 92.2 jit_solution(17138970997936659504)
XLA Ops:
  0.0 89.9 %block.1 = bf16[128,4096]{1,0:T(8,128)(2,1)} custom-call(bf16[128,4096]{1,0:T(8,128)(2,1)} %q.1, bf16[128,4096]{1,0:T(8,128)(2,1)} %k.1, bf16[128,4096]{1,0:T(8,128)(2,1)} %v.1, s32[8,128]{1,0:T(8,128)} %bitcast.7, bf16[128,4096]{1,0:T(8,128)(2,1)} %res.1, f32[1,512]{1,0:T(1,128)} %bitcast.8, f32[1,512]{1,0:T(1,128)} %bitcast.9, bf16[512,4096]{1,0:T(8,128)(2,1)} %w.1, ...), custom_call_target="tpu_custom_call" | custom-call | tf_op jit(solution)/shard_map/block/pallas_call | solution.py:550
  89.9 2.3 %copy.12 = bf16[128,4096]{1,0:T(8,128)(2,1)} copy(bf16[128,4096]{1,0:T(8,128)(2,1)} %block.1) | data formatting | bytes 2097152

commit v3 on v2

v3 whole, which is shorter than its diff:
```python
import jax
import jax.numpy as jnp
from jax import lax
from jax.experimental import pallas as pl
from jax.experimental.pallas import tpu as pltpu
from jax.sharding import PartitionSpec as P

HEAD_DIM = 128
TILE = 128
D = 4096
NY = 4
LATE = NY - 1
FEAT = 1024
NC = 8
CW = FEAT // NC
HALF = NC // 2
EARLY = 3 * NC // 8
WN = 4
WROWS = 128 // WN
JC = 4
COL = 2048 // JC
EXTRA = 16
ROWS = LATE * TILE + EXTRA
WINDOW = (2, 4, 5, 5)
MESH = pl.DeviceIdType.MESH

deep_alpha = 160.0**0.25
LOG2E = 1.4426950408889634
SCALE = LOG2E / HEAD_DIM**0.5


def kernel(
    q, k, v, seg_in, res, gain, bias, w, pg, pb,
    out,
    qb, kb, vb, wb, gb, mask, att, cen, acc, left, left_late, stat, stat_in, vec, pbuf,
    oppb, rel, held, outb, fin, mixed, final, resb, pgb, pbb, seg,
    loc_sem, sent_sem, kv_recv, q_recv, x_recv, l_recv, w_recv, z_recv, o_recv, f_recv, once_recv,
):
    dp = lax.axis_index("dp")
    t = lax.axis_index("tensor")
    core, hi, z = dp % 2, (dp // 2) % 2, dp // 4
    x, y = t % 2, t // 2
    zpar = z % 2

    def y_dev(ty):
        return {"dp": dp, "tensor": ty * 2 + x}

    x_dev = {"dp": dp, "tensor": y * 2 + (1 - x)}
    wrap_dev = {"dp": z * 4 + (1 - hi) * 2 + core, "tensor": y * 2 + (1 - x)}
    core_dev = {"dp": z * 4 + hi * 2 + (1 - core), "tensor": t}
    z_dev = {"dp": (z + 1 - 2 * zpar) * 4 + hi * 2 + core, "tensor": t}
    up, far, down = (y + 1) % NY, (y + 2) % NY, (y + 3) % NY

    def remote(src, dst, ss, rs, dev):
        return pltpu.make_async_remote_copy(
            src_ref=src, dst_ref=dst, send_sem=ss, recv_sem=rs, device_id=dev, device_id_type=MESH
        )

    def wait_bytes(ref, sem):
        pltpu.make_async_copy(ref, ref, sem).wait()

    def rows_at(n, size):
        return pl.ds(pl.multiple_of(n * size, size), size)

    def cols(ty, c):
        return pl.ds(pl.multiple_of(ty * FEAT + c * CW, CW), CW)

    def slot(a, ty, c):
        if a == 0:
            return qb.at[c, rows_at(ty, TILE)]
        return (kb, vb)[a - 1].at[c, rows_at(2 * ty + x, TILE)]

    def y_copy(n, c, a):
        ty = (y + n) % NY
        sem = q_recv if a == 0 else kv_recv
        return remote(
            (q, k, v)[a].at[:, cols(ty, c)], slot(a, y, c), sent_sem.at[0], sem.at[c], y_dev(ty)
        )

    def x_copy(ty, c, a):
        dst = slot(a, ty, c)
        return remote(dst, dst, sent_sem.at[1], x_recv.at[c], x_dev)

    def x_own(c, a):
        return remote(
            (q, k, v)[a].at[:, cols(y, c)], slot(a, y, c), sent_sem.at[1], x_recv.at[c], x_dev
        )

    def l_copy(c, a):
        dst = slot(a, LATE, c)
        return remote(dst, dst, sent_sem.at[2], l_recv.at[c // 2], x_dev)

    def l_own(c, a):
        return remote(
            (q, k, v)[a].at[:, cols(y, c)], slot(a, y, c), sent_sem.at[2], l_recv.at[c // 2], x_dev
        )

    def piece(owner, of_core, of_z, n):
        return wb.at[rows_at(owner * 16 + of_core * 8 + of_z * 4 + n, WROWS)]

    def w_copy(n):
        src = w.at[rows_at(core * 8 + zpar * 4 + n, WROWS)]
        return remote(src, piece(x, core, zpar, n), sent_sem.at[3], w_recv.at[n], wrap_dev)

    def w_wait(n):
        wait_bytes(piece(1 - x, core, zpar, n), w_recv.at[n])

    def z_copy(n):
        src = piece(1 - x, core, zpar, n)
        return remote(src, src, sent_sem.at[3], z_recv.at[n], z_dev)

    def z_wait(n):
        wait_bytes(piece(1 - x, core, 1 - zpar, n), z_recv.at[n])

    def c_copy(of_z, n):
        src = piece(1 - x, core, of_z, n)
        return remote(src, src, sent_sem.at[3], once_recv.at[0], core_dev)

    def g_copy(i):
        return remote((gain, bias)[i], gb.at[i, x], sent_sem.at[4], once_recv.at[1], wrap_dev)

    def s_copy(ty):
        return remote(stat.at[ty], stat_in.at[y], sent_sem.at[5], once_recv.at[2], y_dev(ty))

    def v_copy(n):
        return remote(vec.at[y], vec.at[y], sent_sem.at[6], once_recv.at[3], y_dev((y + n) % NY))

    def o_copy(half, j):
        return remote(
            oppb.at[half, j], rel.at[half, j], sent_sem.at[7], o_recv.at[half, j],
            y_dev((up, down)[half]),
        )

    def f_copy(way, half, j):
        return remote(
            outb.at[way, half, j], fin.at[way, half, j], sent_sem.at[8],
            f_recv.at[half, j], y_dev((up, down)[way]),
        )

    def fetch(src, dst, n):
        return pltpu.make_async_copy(src, dst, loc_sem.at[n])

    fetch_seg = fetch(seg_in, seg, 0)
    fetch_seg.start()

    barrier = pltpu.get_barrier_semaphore()
    peers = [y_dev(up), y_dev(far), y_dev(down), x_dev, wrap_dev, core_dev, z_dev]
    for dev in peers:
        pl.semaphore_signal(barrier, inc=1, device_id=dev, device_id_type=MESH)
    pl.semaphore_wait(barrier, len(peers))

    def send_kv(c, carry):
        for n in (1, 3, 2):
            for a in (1, 2):
                y_copy(n, c, a).start()

        @pl.when(y != LATE)
        def _():
            for a in (1, 2):
                x_own(c, a).start()

        @pl.when((y == LATE) & (x == 0) & (c < EARLY))
        def _():
            for a in (1, 2):
                l_own(c, a).start()

        return carry

    def send_q(c, carry):
        for n in (1, 3, 2):
            y_copy(n, c, 0).start()
        return carry

    lax.fori_loop(0, 1, send_kv, 0)
    for n in range(WN):
        w_copy(n).start()
    lax.fori_loop(1, NC, send_kv, 0)
    for i in range(2):
        g_copy(i).start()
    lax.fori_loop(0, NC, send_q, 0)

    def fetch_own(c, carry):
        for a in range(3):
            fetch((q, k, v)[a].at[:, cols(y, c)], slot(a, y, c), 1).start()
        return carry

    lax.fori_loop(0, NC, fetch_own, 0)
    fetch_gains = [fetch(gain, gb.at[0, x], 2), fetch(bias, gb.at[1, x], 2)]
    fetch_w = fetch(w, wb.at[rows_at(x, 512)], 3)
    fetch_rest = [fetch(pg, pgb, 4), fetch(pb, pbb, 5), fetch(res, resb, 6)]
    for copy in fetch_gains + [fetch_w] + fetch_rest:
        copy.start()

    fetch_seg.wait()

    first_of = (0, 0, x, 2 + x)
    for qi in range(NY):
        tq = 2 * qi + x
        row = seg[pl.ds(tq, 1), :].astype(jnp.float32)
        of_query = jnp.broadcast_to(row, (TILE, TILE)).T
        sub = lax.broadcasted_iota(jnp.int32, (TILE, TILE), 0) + tq * TILE
        lane = lax.broadcasted_iota(jnp.int32, (TILE, TILE), 1)
        for n in range(WINDOW[qi]):
            of_key = seg[pl.ds(first_of[qi] + n, 1), :].astype(jnp.float32)
            seen = (of_query == of_key) & (lane + (first_of[qi] + n) * TILE <= sub)
            mask[qi, :, n * TILE : (n + 1) * TILE] = jnp.where(seen, 0.0, -1e30)

    wait_bytes(kb.at[0:3], loc_sem.at[1])

    def receive_kv(c):
        wait_bytes(kb.at[0, 0 : 6 * TILE], kv_recv.at[c])
        for ty in range(LATE):

            @pl.when(ty != y)
            def _():
                for a in (1, 2):
                    x_copy(ty, c, a).start()

    def spread_z(n):
        z_wait(n)
        c_copy(1 - zpar, n).start()

    def relay(i, carry):
        for h in range(NC // WN):
            receive_kv(i * (NC // WN) + h)
        w_wait(i)
        c_copy(zpar, i).start()
        z_copy(i).start()

        @pl.when(i >= 2)
        def _():
            spread_z(i - 2)

        return carry

    lax.fori_loop(0, WN, relay, 0)

    def relay_late(c, carry):
        @pl.when((x == 0) & ((y != LATE) | (c >= EARLY)))
        def _():
            for a in (1, 2):
                l_copy(c, a).start()

        return carry

    lax.fori_loop(0, NC, relay_late, 0)

    def gains(c):
        return gb[0, c // 4, :, pl.ds(pl.multiple_of((c % 4) * CW, CW), CW)]

    def put(value, c, qi, dst, at, first):
        rows = pl.ds(qi * TILE, TILE)
        value = value - cen[rows, :]
        lanes = pl.ds(pl.multiple_of(c * CW, CW), CW)
        dst[at : at + TILE, lanes] = (value * gains(c)).astype(jnp.bfloat16)
        if first:
            acc[0, rows, :] = value
            acc[1, rows, :] = value * value
        else:
            acc[0, rows, :] += value
            acc[1, rows, :] += value * value

    def attend(c, tiles, dst):
        for qi in tiles:
            n = WINDOW[qi] * TILE
            keys = pl.ds(pl.multiple_of(first_of[qi] * TILE, TILE), n)
            rows = pl.ds(qi * TILE, TILE)
            s = lax.dot_general(
                qb[c, rows, :], kb[c, keys, :], (((1,), (1,)), ((), ())),
                preferred_element_type=jnp.float32,
            )
            s = s + mask[qi, :, :n]
            top = jnp.max(s, axis=-1, keepdims=True)
            p = jnp.exp2((s - top) * SCALE)
            total = jnp.sum(p, axis=-1, keepdims=True)
            o = jnp.dot(
                p.astype(jnp.bfloat16), vb[c, keys, :], preferred_element_type=jnp.float32
            )
            o = o / total
            if dst is None:
                att[c, rows, :] = o
            else:
                put(o, c, qi, dst, (qi - tiles[0]) * TILE, False)

    def center(tiles, dst):
        for qi in tiles:
            rows = pl.ds(qi * TILE, TILE)
            mean = sum(att[c, rows, :] for c in range(HALF))
            mean = jnp.sum(mean, axis=-1, keepdims=True) / (HALF * CW)
            cen[rows, :] = jnp.broadcast_to(mean, (TILE, CW))
            for c in range(HALF):
                put(att[c, rows, :], c, qi, dst, (qi - tiles[0]) * TILE, c == 0)

    def attend_all(tiles, dst, wait):
        def first_half(c, carry):
            wait(c)
            attend(c, tiles, None)
            return carry

        def second_half(c, carry):
            wait(c)
            attend(c, tiles, dst)
            return carry

        lax.fori_loop(0, HALF, first_half, 0)
        center(tiles, dst)
        lax.fori_loop(HALF, NC, second_half, 0)

    def wait_first(c):
        wait_bytes(kb.at[0, 0 : 3 * TILE], q_recv.at[c])
        wait_bytes(kb.at[0, 0 : 6 * TILE], x_recv.at[c])

        @pl.when((c == 2) | (c == 4))
        def _():
            spread_z(1 + c // 2)

    def wait_last(c):
        @pl.when((x == 1) & (c % 2 == 0))
        def _():
            wait_bytes(kb.at[0, 0 : 4 * TILE], l_recv.at[c // 2])

    lane = lax.broadcasted_iota(jnp.int32, (TILE, TILE), 1)

    def statistics(qi):
        rows = pl.ds(qi * TILE, TILE)
        mid = cen[rows, 0:1]
        shift = jnp.sum(acc[0, rows, :], axis=-1, keepdims=True)
        spread = jnp.sum(acc[1, rows, :], axis=-1, keepdims=True) - shift * shift / FEAT
        mean = mid + shift / FEAT
        stat[qi] = jnp.where(lane == 0, mid, jnp.where(lane == 1, mean, spread)).T[:8]

        @pl.when(qi != y)
        def _():
            s_copy(qi).start()

        @pl.when(qi == y)
        def _():
            stat_in[y] = stat[qi]

    for copy in fetch_gains:
        copy.wait()
    wait_bytes(gb.at[:, 0], once_recv.at[1])
    sub = lax.broadcasted_iota(jnp.int32, (EXTRA, CW), 0)
    for c in range(NC):
        half, lanes = c * CW // 512, pl.ds(c * CW % 512, CW)
        value = jnp.zeros((EXTRA, CW), jnp.float32)
        for i in range(2):
            row = gb[i, half, :, lanes]
            high = row.astype(jnp.bfloat16).astype(jnp.float32)
            value = jnp.where(sub == 2 * i, high, jnp.where(sub == 2 * i + 1, row - high, value))
        left[LATE * TILE : ROWS, c * CW : (c + 1) * CW] = value.astype(jnp.bfloat16)

    attend_all(range(LATE), left, wait_first)

    fetch_w.wait()
    wait_bytes(kb, once_recv.at[0])

    def col(half, j):
        return pl.ds(pl.multiple_of(half * 2048 + j * COL, COL), COL)

    def hand_out(role, half, j, rows, start):
        value = pbuf[rows, :]
        if role == 2:
            oppb[half, j] = value.astype(jnp.bfloat16)
            o_copy(half, j).start()
        elif role == 0:
            mixed[half, j] = value
        else:
            way = 0 if role == 1 else 1
            if half == way:
                held[half, j] = value
            else:
                outb[way, half, j] = value.astype(jnp.bfloat16)
                if start:
                    f_copy(way, half, j).start()

    def project(j, carry):
        for half in range(2):
            pbuf[...] = jnp.dot(left[...], wb[:, col(half, j)], preferred_element_type=jnp.float32)
            for role in (2, 1, 3, 0):
                ty = (y + role) % NY

                @pl.when(ty != LATE)
                def _():
                    hand_out(role, half, j, rows_at(ty, TILE), False)

            extra = pbuf[LATE * TILE : ROWS, :]
            vec[y, 0, :, col(half, j)] = extra[0:1] + extra[1:2]
            vec[y, 1, :, col(half, j)] = extra[2:3] + extra[3:4]
        return carry

    lax.fori_loop(0, JC, project, 0)

    def send_direct(j, carry):
        @pl.when(up != LATE)
        def _():
            f_copy(0, 1, j).start()

        @pl.when(down != LATE)
        def _():
            f_copy(1, 0, j).start()

        return carry

    lax.fori_loop(0, JC, send_direct, 0)
    for n in (1, 3, 2):
        v_copy(n).start()
    for qi in range(LATE):
        statistics(qi)

    attend_all((LATE,), left_late, wait_last)

    def project_late(j, carry):
        for half in range(2):
            pbuf[:TILE] = jnp.dot(
                left_late[...], wb[:, col(half, j)], preferred_element_type=jnp.float32
            )
            for role in (2, 1, 3, 0):

                @pl.when((y + role) % NY == LATE)
                def _():
                    hand_out(role, half, j, pl.ds(0, TILE), True)

        return carry

    lax.fori_loop(0, JC, project_late, 0)

    statistics(LATE)
    wait_bytes(wb.at[0:288], sent_sem.at[0])
    wait_bytes(kb.at[0:6], sent_sem.at[1])

    @pl.when(x == 0)
    def _():
        wait_bytes(kb.at[0:2], sent_sem.at[2])

    wait_bytes(wb.at[0:512], sent_sem.at[3])
    wait_bytes(gb.at[:, 0], sent_sem.at[4])
    wait_bytes(stat.at[0:3], sent_sem.at[5])
    wait_bytes(vec.at[0:3], sent_sem.at[6])

    def pass_on(half, j):
        wait_bytes(rel.at[half, j], o_recv.at[half, j])
        value = held[half, j] + rel[half, j].astype(jnp.float32)
        outb[half, half, j] = value.astype(jnp.bfloat16)
        f_copy(half, half, j).start()

    def pass_first(j, carry):
        for half in range(2):

            @pl.when((up, down)[half] != LATE)
            def _():
                pass_on(half, j)

        return carry

    def pass_late(j, carry):
        for half in range(2):

            @pl.when((up, down)[half] == LATE)
            def _():
                pass_on(half, j)

        return carry

    lax.fori_loop(0, JC, pass_first, 0)
    lax.fori_loop(0, JC, pass_late, 0)

    wait_bytes(stat_in.at[0:3], once_recv.at[2])
    wait_bytes(vec.at[0:3], once_recv.at[3])
    for copy in fetch_rest:
        copy.wait()

    means = [stat_in[ty, 1:2, :] for ty in range(NY)]
    mean = sum(means) / NY
    spread = sum(stat_in[ty, 2:3, :] for ty in range(NY))
    spread = spread + FEAT * sum((m - mean) ** 2 for m in means)
    inv = lax.rsqrt(spread / (NY * FEAT) + 1e-05)
    sub = lax.broadcasted_iota(jnp.int32, (TILE, TILE), 0)
    both = jnp.broadcast_to(inv, (TILE, TILE))
    for ty in range(NY):
        both = jnp.where(sub == ty, stat_in[ty, 0:1, :] - mean, both)
    both = both.T
    inv = both[:, NY : NY + 1]

    def prepare(j, carry):
        for half in range(2):
            value = mixed[half, j]
            shift = jnp.zeros((1, COL), jnp.float32)
            for ty in range(NY):
                value = value + both[:, ty : ty + 1] * vec[ty, 0, :, col(half, j)]
                shift = shift + vec[ty, 1, :, col(half, j)]
            stream = deep_alpha * resb[:, col(half, j)].astype(jnp.float32)
            mixed[half, j] = value * inv + shift + stream
        return carry

    lax.fori_loop(0, JC, prepare, 0)

    def m_copy(half, j):
        return pltpu.make_async_copy(
            final.at[half, j], out.at[:, col(half, j)], loc_sem.at[7]
        )

    def collect(j, total):
        for half in range(2):
            wait_bytes(fin.at[:, half, j], f_recv.at[half, j])
            value = fin[0, half, j].astype(jnp.float32) + fin[1, half, j].astype(jnp.float32)
            value = mixed[half, j] + inv * value
            mixed[half, j] = value
            total = total + jnp.sum(value, axis=-1, keepdims=True)
        return total

    total = lax.fori_loop(0, JC, collect, jnp.zeros((TILE, 1), jnp.float32))
    mean = total / D
    spread = jnp.zeros((TILE, 1), jnp.float32)
    for half in range(2):
        for j in range(JC):
            spread = spread + jnp.sum((mixed[half, j] - mean) ** 2, axis=-1, keepdims=True)
    inv = lax.rsqrt(spread / D + 1e-05)
    for half in range(2):
        for j in range(JC):
            lanes = pl.ds(half * 2048 + j * COL, COL)
            value = (mixed[half, j] - mean) * inv * pgb[:, lanes] + pbb[:, lanes]
            final[half, j] = value.astype(jnp.bfloat16)
            m_copy(half, j).start()
    wait_bytes(final, loc_sem.at[7])
    wait_bytes(oppb, sent_sem.at[7])
    wait_bytes(outb, sent_sem.at[8])


def body(
    queries, keys, values, segment_ids, residual, sub_gain, sub_bias, out_weight, post_gain, post_bias
):
    any_spec = pl.BlockSpec(memory_space=pl.ANY)
    bf16, f32 = jnp.bfloat16, jnp.float32
    dma = pltpu.SemaphoreType.DMA
    return pl.pallas_call(
        kernel,
        name="block",
        out_shape=jax.ShapeDtypeStruct((TILE, D), bf16),
        in_specs=[any_spec] * 10,
        out_specs=any_spec,
        scratch_shapes=[
            pltpu.VMEM((NC, NY * TILE, CW), bf16),
            pltpu.VMEM((NC, 8 * TILE, CW), bf16),
            pltpu.VMEM((NC, 8 * TILE, CW), bf16),
            pltpu.VMEM((FEAT, D), bf16),
            pltpu.VMEM((2, 2, 1, 512), f32),
            pltpu.VMEM((NY, TILE, 5 * TILE), f32),
            pltpu.VMEM((HALF, NY * TILE, CW), f32),
            pltpu.VMEM((NY * TILE, CW), f32),
            pltpu.VMEM((2, NY * TILE, CW), f32),
            pltpu.VMEM((ROWS, FEAT), bf16),
            pltpu.VMEM((TILE, FEAT), bf16),
            pltpu.VMEM((NY, 8, TILE), f32),
            pltpu.VMEM((NY, 8, TILE), f32),
            pltpu.VMEM((NY, 2, 1, D), f32),
            pltpu.VMEM((ROWS, COL), f32),
            pltpu.VMEM((2, JC, TILE, COL), bf16),
            pltpu.VMEM((2, JC, TILE, COL), bf16),
            pltpu.VMEM((2, JC, TILE, COL), f32),
            pltpu.VMEM((2, 2, JC, TILE, COL), bf16),
            pltpu.VMEM((2, 2, JC, TILE, COL), bf16),
            pltpu.VMEM((2, JC, TILE, COL), f32),
            pltpu.VMEM((2, JC, TILE, COL), bf16),
            pltpu.VMEM((TILE, D), bf16),
            pltpu.VMEM((1, D), f32),
            pltpu.VMEM((1, D), f32),
            pltpu.VMEM((8, TILE), jnp.int32),
            dma((8,)),
            dma((9,)),
            dma((NC,)),
            dma((NC,)),
            dma((NC,)),
            dma((NC // 2,)),
            dma((WN,)),
            dma((WN,)),
            dma((2, JC)),
            dma((2, JC)),
            dma((4,)),
        ],
        compiler_params=pltpu.CompilerParams(
            collective_id=0, has_side_effects=True, vmem_limit_bytes=56 << 20
        ),
    )(
        queries,
        keys,
        values,
        segment_ids.reshape(8, TILE),
        residual,
        sub_gain.reshape(1, 512),
        sub_bias.reshape(1, 512),
        out_weight,
        post_gain.reshape(1, D),
        post_bias.reshape(1, D),
    )


def solution(mesh):
    return jax.shard_map(
        body,
        mesh=mesh,
        in_specs=(
            P(("dp", "tensor"), None),
            P(("dp", "tensor"), None),
            P(("dp", "tensor"), None),
            P("dp"),
            P(("dp", "tensor"), None),
            P("tensor"),
            P("tensor"),
            P("tensor", None),
            P(),
            P(),
        ),
        out_specs=P(("dp", "tensor"), None),
        check_vma=False,
    )
```

time: 92.4 us -> 86.7 us (0.938)
  Pallas kernels: 89.9 us -> 84.3 us
    pallas_call x1, Pallas kernels: 89.9 us -> 84.3 us  [body(): pl.pallas_call(kernel, name='block', out_shape=jax.ShapeDtypeStruct((TILE...]
where the time goes in v3:
time: 86.7 us; the launch traced here: 86.6 us
  Pallas kernels  84.3 us (97%)
  local copies, waits for them, and re-layouts  2.29 us (3%)
    pallas_call x1, Pallas kernels, body(): pl.pallas_call(kernel, name='block', out_shape=jax.ShapeDtypeStruct((TILE...  84.3 us
    unnamed x1, local copies, waits for them, and re-layouts  2.29 us

profile of v3, /device:TPU:32, one launch (start us, length us, event | category | flops | bytes accessed | tf_op | source)
XLA Modules:
  0.0 86.6 jit_solution(17220205881339017115)
XLA Ops:
  0.0 84.3 %block.1 = bf16[128,4096]{1,0:T(8,128)(2,1)} custom-call(bf16[128,4096]{1,0:T(8,128)(2,1)} %q.1, bf16[128,4096]{1,0:T(8,128)(2,1)} %k.1, bf16[128,4096]{1,0:T(8,128)(2,1)} %v.1, s32[8,128]{1,0:T(8,128)} %bitcast.7, bf16[128,4096]{1,0:T(8,128)(2,1)} %res.1, f32[1,512]{1,0:T(1,128)} %bitcast.8, f32[1,512]{1,0:T(1,128)} %bitcast.9, bf16[512,4096]{1,0:T(8,128)(2,1)} %w.1, ...), custom_call_target="tpu_custom_call" | custom-call | tf_op jit(solution)/shard_map/block/pallas_call | solution.py:536
  84.3 2.3 %copy.12 = bf16[128,4096]{1,0:T(8,128)(2,1)} copy(bf16[128,4096]{1,0:T(8,128)(2,1)} %block.1) | data formatting | bytes 2097152

commit v4 on v3

--- a/solution.py
+++ b/solution.py
@@ -32,7 +32,7 @@
 def kernel(
     q, k, v, seg_in, res, gain, bias, w, pg, pb,
     out,
-    qb, kb, vb, wb, gb, mask, att, cen, acc, left, left_late, stat, stat_in, vec, pbuf,
+    qs, ks, vs, qb, kb, vb, wb, gb, mask, att, cen, acc, left, left_late, stat, stat_in, vec, pbuf,
     oppb, rel, held, outb, fin, mixed, final, resb, pgb, pbb, seg,
     loc_sem, sent_sem, kv_recv, q_recv, x_recv, l_recv, w_recv, z_recv, o_recv, f_recv, once_recv,
 ):
@@ -74,7 +74,7 @@
         ty = (y + n) % NY
         sem = q_recv if a == 0 else kv_recv
         return remote(
-            (q, k, v)[a].at[:, cols(ty, c)], slot(a, y, c), sent_sem.at[0], sem.at[c], y_dev(ty)
+            (qs, ks, vs)[a].at[:, cols(ty, c)], slot(a, y, c), sent_sem.at[0], sem.at[c], y_dev(ty)
         )
 
     def x_copy(ty, c, a):
@@ -83,7 +83,7 @@
 
     def x_own(c, a):
         return remote(
-            (q, k, v)[a].at[:, cols(y, c)], slot(a, y, c), sent_sem.at[1], x_recv.at[c], x_dev
+            (qs, ks, vs)[a].at[:, cols(y, c)], slot(a, y, c), sent_sem.at[1], x_recv.at[c], x_dev
         )
 
     def l_copy(c, a):
@@ -92,7 +92,7 @@
 
     def l_own(c, a):
         return remote(
-            (q, k, v)[a].at[:, cols(y, c)], slot(a, y, c), sent_sem.at[2], l_recv.at[c // 2], x_dev
+            (qs, ks, vs)[a].at[:, cols(y, c)], slot(a, y, c), sent_sem.at[2], l_recv.at[c // 2], x_dev
         )
 
     def piece(owner, of_core, of_z, n):
@@ -140,6 +140,9 @@
     def fetch(src, dst, n):
         return pltpu.make_async_copy(src, dst, loc_sem.at[n])
 
+    stage = [fetch((q, k, v)[a], (qs, ks, vs)[a], 8 + a) for a in range(3)]
+    for a in (1, 2, 0):
+        stage[a].start()
     fetch_seg = fetch(seg_in, seg, 0)
     fetch_seg.start()
 
@@ -150,8 +153,8 @@
     pl.semaphore_wait(barrier, len(peers))
 
     def send_kv(c, carry):
-        for n in (1, 3, 2):
-            for a in (1, 2):
+        for a in (1, 2):
+            for n in (1, 3, 2):
                 y_copy(n, c, a).start()
 
         @pl.when(y != LATE)
@@ -171,17 +174,20 @@
             y_copy(n, c, 0).start()
         return carry
 
+    stage[1].wait()
+    stage[2].wait()
     lax.fori_loop(0, 1, send_kv, 0)
     for n in range(WN):
         w_copy(n).start()
     lax.fori_loop(1, NC, send_kv, 0)
     for i in range(2):
         g_copy(i).start()
+    stage[0].wait()
     lax.fori_loop(0, NC, send_q, 0)
 
     def fetch_own(c, carry):
         for a in range(3):
-            fetch((q, k, v)[a].at[:, cols(y, c)], slot(a, y, c), 1).start()
+            fetch((qs, ks, vs)[a].at[:, cols(y, c)], slot(a, y, c), 1).start()
         return carry
 
     lax.fori_loop(0, NC, fetch_own, 0)
@@ -358,7 +364,12 @@
     def col(half, j):
         return pl.ds(pl.multiple_of(half * 2048 + j * COL, COL), COL)
 
-    def hand_out(role, half, j, rows, start):
+    def vec_at(i, half, j):
+        at = j * COL
+        lanes = pl.ds(pl.multiple_of(at % 1024, COL), COL)
+        return pl.ds(i * 4 + half * 2 + at // 1024, 1), lanes
+
+    def hand_out(role, half, j, rows, at_once):
         value = pbuf[rows, :]
         if role == 2:
             oppb[half, j] = value.astype(jnp.bfloat16)
@@ -371,7 +382,9 @@
                 held[half, j] = value
             else:
                 outb[way, half, j] = value.astype(jnp.bfloat16)
-                if start:
+
+                @pl.when(at_once)
+                def _():
                     f_copy(way, half, j).start()
 
     def project(j, carry):
@@ -382,21 +395,22 @@
 
                 @pl.when(ty != LATE)
                 def _():
-                    hand_out(role, half, j, rows_at(ty, TILE), False)
+                    hand_out(role, half, j, rows_at(ty, TILE), far == LATE)
 
             extra = pbuf[LATE * TILE : ROWS, :]
-            vec[y, 0, :, col(half, j)] = extra[0:1] + extra[1:2]
-            vec[y, 1, :, col(half, j)] = extra[2:3] + extra[3:4]
+            for i in range(2):
+                row, lanes = vec_at(i, half, j)
+                vec[y, row, lanes] = extra[2 * i : 2 * i + 1] + extra[2 * i + 1 : 2 * i + 2]
         return carry
 
     lax.fori_loop(0, JC, project, 0)
 
     def send_direct(j, carry):
-        @pl.when(up != LATE)
+        @pl.when((up != LATE) & (far != LATE))
         def _():
             f_copy(0, 1, j).start()
 
-        @pl.when(down != LATE)
+        @pl.when((down != LATE) & (far != LATE))
         def _():
             f_copy(1, 0, j).start()
 
@@ -407,6 +421,23 @@
         v_copy(n).start()
     for qi in range(LATE):
         statistics(qi)
+
+    def pass_on(half, j):
+        wait_bytes(rel.at[half, j], o_recv.at[half, j])
+        value = held[half, j] + rel[half, j].astype(jnp.float32)
+        outb[half, half, j] = value.astype(jnp.bfloat16)
+        f_copy(half, half, j).start()
+
+    def pass_first(j, carry):
+        for half in range(2):
+
+            @pl.when((up, down)[half] != LATE)
+            def _():
+                pass_on(half, j)
+
+        return carry
+
+    lax.fori_loop(0, JC // 2, pass_first, 0)
 
     attend_all((LATE,), left_late, wait_last)
 
@@ -419,7 +450,7 @@
 
                 @pl.when((y + role) % NY == LATE)
                 def _():
-                    hand_out(role, half, j, pl.ds(0, TILE), True)
+                    hand_out(role, half, j, pl.ds(0, TILE), y >= 0)
 
         return carry
 
@@ -438,21 +469,6 @@
     wait_bytes(stat.at[0:3], sent_sem.at[5])
     wait_bytes(vec.at[0:3], sent_sem.at[6])
 
-    def pass_on(half, j):
-        wait_bytes(rel.at[half, j], o_recv.at[half, j])
-        value = held[half, j] + rel[half, j].astype(jnp.float32)
-        outb[half, half, j] = value.astype(jnp.bfloat16)
-        f_copy(half, half, j).start()
-
-    def pass_first(j, carry):
-        for half in range(2):
-
-            @pl.when((up, down)[half] != LATE)
-            def _():
-                pass_on(half, j)
-
-        return carry
-
     def pass_late(j, carry):
         for half in range(2):
 
@@ -462,7 +478,7 @@
 
         return carry
 
-    lax.fori_loop(0, JC, pass_first, 0)
+    lax.fori_loop(JC // 2, JC, pass_first, 0)
     lax.fori_loop(0, JC, pass_late, 0)
 
     wait_bytes(stat_in.at[0:3], once_recv.at[2])
@@ -487,8 +503,10 @@
             value = mixed[half, j]
             shift = jnp.zeros((1, COL), jnp.float32)
             for ty in range(NY):
-                value = value + both[:, ty : ty + 1] * vec[ty, 0, :, col(half, j)]
-                shift = shift + vec[ty, 1, :, col(half, j)]
+                row, lanes = vec_at(0, half, j)
+                value = value + both[:, ty : ty + 1] * vec[ty, row, lanes]
+                row, lanes = vec_at(1, half, j)
+                shift = shift + vec[ty, row, lanes]
             stream = deep_alpha * resb[:, col(half, j)].astype(jnp.float32)
             mixed[half, j] = value * inv + shift + stream
         return carry
@@ -500,21 +518,28 @@
             final.at[half, j], out.at[:, col(half, j)], loc_sem.at[7]
         )
 
-    def collect(j, total):
+    def arrive(half, j):
+        wait_bytes(fin.at[:, half, j], f_recv.at[half, j])
+        value = fin[0, half, j].astype(jnp.float32) + fin[1, half, j].astype(jnp.float32)
+        value = mixed[half, j] + inv * value
+        mixed[half, j] = value
+        return value
+
+    start = [arrive(half, 0) for half in range(2)]
+    mid = sum(jnp.sum(value, axis=-1, keepdims=True) for value in start) / (2 * COL)
+    spread = sum(jnp.sum((value - mid) ** 2, axis=-1, keepdims=True) for value in start)
+
+    def collect(j, carry):
+        total, spread = carry
         for half in range(2):
-            wait_bytes(fin.at[:, half, j], f_recv.at[half, j])
-            value = fin[0, half, j].astype(jnp.float32) + fin[1, half, j].astype(jnp.float32)
-            value = mixed[half, j] + inv * value
-            mixed[half, j] = value
+            value = arrive(half, j) - mid
             total = total + jnp.sum(value, axis=-1, keepdims=True)
-        return total
-
-    total = lax.fori_loop(0, JC, collect, jnp.zeros((TILE, 1), jnp.float32))
-    mean = total / D
-    spread = jnp.zeros((TILE, 1), jnp.float32)
-    for half in range(2):
-        for j in range(JC):
-            spread = spread + jnp.sum((mixed[half, j] - mean) ** 2, axis=-1, keepdims=True)
+            spread = spread + jnp.sum(value * value, axis=-1, keepdims=True)
+        return total, spread
+
+    total, spread = lax.fori_loop(1, JC, collect, (jnp.zeros((TILE, 1), jnp.float32), spread))
+    mean = mid + total / D
+    spread = spread - total * total / D
     inv = lax.rsqrt(spread / D + 1e-05)
     for half in range(2):
         for j in range(JC):
@@ -540,6 +565,9 @@
         in_specs=[any_spec] * 10,
         out_specs=any_spec,
         scratch_shapes=[
+            pltpu.VMEM((TILE, D), bf16),
+            pltpu.VMEM((TILE, D), bf16),
+            pltpu.VMEM((TILE, D), bf16),
             pltpu.VMEM((NC, NY * TILE, CW), bf16),
             pltpu.VMEM((NC, 8 * TILE, CW), bf16),
             pltpu.VMEM((NC, 8 * TILE, CW), bf16),
@@ -553,7 +581,7 @@
             pltpu.VMEM((TILE, FEAT), bf16),
             pltpu.VMEM((NY, 8, TILE), f32),
             pltpu.VMEM((NY, 8, TILE), f32),
-            pltpu.VMEM((NY, 2, 1, D), f32),
+            pltpu.VMEM((NY, 8, D // 4), f32),
             pltpu.VMEM((ROWS, COL), f32),
             pltpu.VMEM((2, JC, TILE, COL), bf16),
             pltpu.VMEM((2, JC, TILE, COL), bf16),
@@ -566,7 +594,7 @@
             pltpu.VMEM((1, D), f32),
             pltpu.VMEM((1, D), f32),
             pltpu.VMEM((8, TILE), jnp.int32),
-            dma((8,)),
+            dma((11,)),
             dma((9,)),
             dma((NC,)),
             dma((NC,)),

time: 86.7 us -> 85.3 us (0.984)
  Pallas kernels: 84.3 us -> 82.7 us
    pallas_call x1, Pallas kernels: 84.3 us -> 82.7 us  [body(): pl.pallas_call(kernel, name='block', out_shape=jax.ShapeDtypeStruct((TILE...]
where the time goes in v4:
time: 85.3 us; the launch traced here: 85 us
  Pallas kernels  82.7 us (97%)
  local copies, waits for them, and re-layouts  2.29 us (3%)
    pallas_call x1, Pallas kernels, body(): pl.pallas_call(kernel, name='block', out_shape=jax.ShapeDtypeStruct((TILE...  82.7 us
    unnamed x1, local copies, waits for them, and re-layouts  2.29 us

profile of v4, /device:TPU:32, one launch (start us, length us, event | category | flops | bytes accessed | tf_op | source)
XLA Modules:
  0.0 85.0 jit_solution(9795863820305240565)
XLA Ops:
  0.0 82.7 %block.1 = bf16[128,4096]{1,0:T(8,128)(2,1)} custom-call(bf16[128,4096]{1,0:T(8,128)(2,1)} %q.1, bf16[128,4096]{1,0:T(8,128)(2,1)} %k.1, bf16[128,4096]{1,0:T(8,128)(2,1)} %v.1, s32[8,128]{1,0:T(8,128)} %bitcast.7, bf16[128,4096]{1,0:T(8,128)(2,1)} %res.1, f32[1,512]{1,0:T(1,128)} %bitcast.8, f32[1,512]{1,0:T(1,128)} %bitcast.9, bf16[512,4096]{1,0:T(8,128)(2,1)} %w.1, ...), custom_call_target="tpu_custom_call" | custom-call | tf_op jit(solution)/shard_map/block/pallas_call | solution.py:561
  82.7 2.3 %copy.12 = bf16[128,4096]{1,0:T(8,128)(2,1)} copy(bf16[128,4096]{1,0:T(8,128)(2,1)} %block.1) | data formatting | bytes 2097152

commit v5 on v4

--- a/solution.py
+++ b/solution.py
@@ -466,8 +466,6 @@
 
     wait_bytes(wb.at[0:512], sent_sem.at[3])
     wait_bytes(gb.at[:, 0], sent_sem.at[4])
-    wait_bytes(stat.at[0:3], sent_sem.at[5])
-    wait_bytes(vec.at[0:3], sent_sem.at[6])
 
     def pass_late(j, carry):
         for half in range(2):
@@ -548,6 +546,8 @@
             final[half, j] = value.astype(jnp.bfloat16)
             m_copy(half, j).start()
     wait_bytes(final, loc_sem.at[7])
+    wait_bytes(stat.at[0:3], sent_sem.at[5])
+    wait_bytes(vec.at[0:3], sent_sem.at[6])
     wait_bytes(oppb, sent_sem.at[7])
     wait_bytes(outb, sent_sem.at[8])
 

time: 85.3 us -> 85.1 us (level)
  no operation moved by 1% of the time
where the time goes in v5:
time: 85.1 us; the launch traced here: 85 us
  Pallas kernels  82.7 us (97%)
  local copies, waits for them, and re-layouts  2.29 us (3%)
    pallas_call x1, Pallas kernels, body(): pl.pallas_call(kernel, name='block', out_shape=jax.ShapeDtypeStruct((TILE...  82.7 us
    unnamed x1, local copies, waits for them, and re-layouts  2.29 us

profile of v5, /device:TPU:32, one launch (start us, length us, event | category | flops | bytes accessed | tf_op | source)
XLA Modules:
  0.0 85.0 jit_solution(13962112398449667783)
XLA Ops:
  0.0 82.7 %block.1 = bf16[128,4096]{1,0:T(8,128)(2,1)} custom-call(bf16[128,4096]{1,0:T(8,128)(2,1)} %q.1, bf16[128,4096]{1,0:T(8,128)(2,1)} %k.1, bf16[128,4096]{1,0:T(8,128)(2,1)} %v.1, s32[8,128]{1,0:T(8,128)} %bitcast.7, bf16[128,4096]{1,0:T(8,128)(2,1)} %res.1, f32[1,512]{1,0:T(1,128)} %bitcast.8, f32[1,512]{1,0:T(1,128)} %bitcast.9, bf16[512,4096]{1,0:T(8,128)(2,1)} %w.1, ...), custom_call_target="tpu_custom_call" | custom-call | tf_op jit(solution)/shard_map/block/pallas_call | solution.py:561
  82.7 2.3 %copy.12 = bf16[128,4096]{1,0:T(8,128)(2,1)} copy(bf16[128,4096]{1,0:T(8,128)(2,1)} %block.1) | data formatting | bytes 2097152
